TPU v7x, 512 devices: a whole 4x8x8 slice. The times are simulated.
512 devices in a mesh: al: 32 (over y, x), ka: 16 (over z, core).
Axes of the slice: x: 4, y: 8, z: 8, core: 2. Of those that a mesh axis runs over, the one named last changes fastest.
Arguments:
- amplitudes: float32 [128, 2048, 128], P('al', 'ka'), may hold values from -6 to 6
- kernel: bfloat16 [128, 2048, 2048], P('al', 'ka'), as said below
- block_lengths: int32 [32], P('al'), may hold values from 1 to 4, 64 in all
- m_counts: int32 [64], replicated, may hold values from 1 to 64, as said below
- vector_potential: float32 [2, 2], replicated, may hold values from -2 to 2
Outputs:
- advanced: float32 [128, 2048, 128], P('al', 'ka')
Inputs may be any that keep to these rules, and one draw needn't show every extreme that they name: `block_lengths`: the lengths sum to 64; one of them equals 4. `m_counts`: the count of partial wave l is at most 2 l + 1; the last partial wave has the largest count. Each slot's kernel is exactly symmetric in its two momenta.
All inputs are finite; a program needn't handle non-finite values. No bound on the sum of `block_lengths` on one device may be relied on, other than what follows from the above.
Results may differ from a plain program's by a relative error of at most 0.007.
Values may be sent and summed in bfloat16 or wider, within the bound.
No kernel may reach another device: no remote copies, remote signals or barrier semaphores. Data moves between devices by JAX's collectives and lax.ppermute only.
A program may use at most 64 MiB of HBM per device.

v0:
```python
import jax
import jax.numpy as jnp
from jax import lax
from jax.sharding import PartitionSpec as P

step_length = 0.2
momentum_top = 3.0


def entering(value, axis, join, neutral):
    count, mine = (lax.axis_size(axis), lax.axis_index(axis))
    pieces = lax.all_gather(value, axis)
    total = jnp.full_like(value, 0) + jnp.asarray(neutral, value.dtype)

    def turn(position, total):
        longer = join(total, pieces[position])
        return jnp.where(position < mine, longer, total)

    return lax.fori_loop(0, count - 1, turn, total)


def shortened(x):

    def short(part):
        return part.astype(jnp.bfloat16) if part.dtype == jnp.float32 else part

    return jax.tree.map(short, x)


def passed_along(block, axis, distance):
    devices = range(lax.axis_size(axis))
    route = [(i - distance, i) for i in devices if i - distance in devices]
    return lax.ppermute(block, axis, route)


def raising(upper_wave, lower_wave, m_low):
    lower_float = lower_wave.astype(jnp.float32)
    m_float = m_low.astype(jnp.float32)
    plus_term = (
        (lower_float + m_float + 1.0)
        * (lower_float + m_float + 2.0)
        / jnp.maximum((2.0 * lower_float + 1.0) * (2.0 * lower_float + 3.0), 1.0)
    )
    minus_term = jnp.maximum(
        (lower_float - m_float) * (lower_float - m_float - 1.0), 0.0
    ) / jnp.maximum((2.0 * lower_float - 1.0) * (2.0 * lower_float + 1.0), 1.0)
    return jnp.where(
        upper_wave == lower_wave + 1,
        jnp.sqrt(jnp.maximum(plus_term, 0.0)),
        jnp.where(upper_wave == lower_wave - 1, -jnp.sqrt(minus_term), 0.0),
    )


def mix_block(
    wave_target, wave_source, count_target, count_source, field_x, field_y, mslots, lcount
):
    target = jnp.arange(mslots, dtype=jnp.int32)[:, None]
    source = jnp.arange(mslots, dtype=jnp.int32)[None, :]
    m_target = target - (count_target - 1) // 2
    m_source = source - (count_source - 1) // 2
    allowed = (
        (target < count_target)
        & (source < count_source)
        & (wave_source >= 0)
        & (wave_source < lcount)
    )
    raise_part = jnp.where(
        allowed & (m_target == m_source + 1), raising(wave_target, wave_source, m_source), 0.0
    )
    lower_part = jnp.where(
        allowed & (m_target == m_source - 1), raising(wave_source, wave_target, m_target), 0.0
    )
    real_part = 0.5 * field_x * (raise_part + lower_part)
    imag_part = 0.5 * field_y * (lower_part - raise_part)
    top_half = jnp.concatenate([real_part.T, imag_part.T], axis=1)
    bottom_half = jnp.concatenate([-imag_part.T, real_part.T], axis=1)
    return jnp.concatenate([top_half, bottom_half], axis=0)


def add_ints(earlier, later):
    return earlier + later


def lookup(lookup_table, wanted):
    entries = jnp.arange(lookup_table.shape[0], dtype=jnp.int32)
    return jnp.sum(jnp.where(wanted[:, None] == entries[None, :], lookup_table[None, :], 0), axis=1)


def shards(amplitudes, kernel, block_lengths, m_counts, vector_potential):
    slot_count, row_count, lane_number = amplitudes.shape
    radial_count = kernel.shape[2]
    mslots = lane_number // 2
    lcount = m_counts.shape[0]
    block_total = lax.axis_size("ka")
    held_waves = block_lengths[0]
    first_wave = entering(block_lengths, "al", add_ints, jnp.zeros((1,), jnp.int32))[0]
    positions = jnp.arange(slot_count, dtype=jnp.int32)
    wave_ids = first_wave + positions
    occupied = positions < held_waves
    counts = lookup(m_counts, wave_ids)
    below_counts = lookup(m_counts, wave_ids - 1)
    above_counts = lookup(m_counts, wave_ids + 1)
    lane_slot = jnp.arange(lane_number, dtype=jnp.int32) % mslots
    lane_keep = ((lane_slot[None, :] < counts[:, None]) & occupied[:, None]).astype(jnp.float32)[
        :, None, :
    ]
    row_start = lax.axis_index("ka") * row_count
    momenta = (row_start + jnp.arange(row_count, dtype=jnp.float32) + 0.5) * (
        momentum_top / radial_count
    )
    build = jax.vmap(mix_block, in_axes=(0, 0, 0, 0, None, None, None, None))
    start_state = amplitudes * lane_keep

    def kernel_apply(rounded):
        gathered = lax.all_gather(rounded, "ka", axis=1, tiled=True)
        state_blocks = gathered.reshape(slot_count, block_total, row_count, lane_number)
        kernel_blocks = kernel.reshape(slot_count, row_count, block_total, row_count)
        parts = jnp.einsum(
            "jrbk,jbkn->jbrn", kernel_blocks, state_blocks, preferred_element_type=jnp.float32
        )
        parts = lax.optimization_barrier(parts.astype(jnp.bfloat16)).astype(jnp.float32)
        return jnp.sum(parts, axis=1)

    def time_derivative(current, field_x, field_y):
        kernel_term = kernel_apply(current.astype(jnp.bfloat16))
        last_slot = lax.dynamic_index_in_dim(current, held_waves - 1, 0, keepdims=False)
        from_below = passed_along(shortened(last_slot), "al", 1).astype(last_slot.dtype)
        from_above = passed_along(shortened(current[0]), "al", -1)
        below_state = jnp.concatenate([from_below[None], current[:-1]], axis=0)
        shifted_up = jnp.concatenate([current[1:], jnp.zeros_like(current[:1])], axis=0)
        above_state = jnp.where(
            (positions + 1 < held_waves)[:, None, None], shifted_up, from_above[None]
        )
        lower_mix = build(
            wave_ids, wave_ids - 1, counts, below_counts, field_x, field_y, mslots, lcount
        )
        upper_mix = build(
            wave_ids, wave_ids + 1, counts, above_counts, field_x, field_y, mslots, lcount
        )
        coupled = jnp.einsum(
            "jrn,jnp->jrp", below_state, lower_mix, precision=lax.Precision.HIGHEST
        )
        coupled = coupled + jnp.einsum(
            "jrn,jnp->jrp", above_state, upper_mix, precision=lax.Precision.HIGHEST
        )
        hamiltonian = (
            0.5 * (momenta * momenta)[None, :, None] * current
            + kernel_term
            + momenta[None, :, None] * coupled
        )
        return jnp.concatenate([hamiltonian[..., mslots:], -hamiltonian[..., :mslots]], axis=-1)

    half_state = start_state + 0.5 * step_length * time_derivative(
        start_state, vector_potential[0, 0], vector_potential[0, 1]
    )
    ending_state = start_state + step_length * time_derivative(
        half_state, vector_potential[1, 0], vector_potential[1, 1]
    )
    return ending_state * lane_keep


def solution(mesh):
    in_specs = (P("al", "ka", None), P("al", "ka", None), P("al"), P(), P())
    out_specs = P("al", "ka", None)
    return jax.shard_map(shards, mesh=mesh, in_specs=in_specs, out_specs=out_specs, check_vma=False)
```

profile of v0, /device:TPU:57, one launch (start us, length us, event | category | flops | bytes accessed | tf_op | source)
XLA Modules:
  0.0 180.6 jit_solution(15269068890538727783)
XLA Ops:
  7.3 1.4 dynamic-slice
  8.7 0.8 dynamic-update-slice
  9.5 12.9 %all-reduce.2 = s32[32]{0:T(128)S(1)} all-reduce(s32[32]{0:T(128)S(1)} %dynamic-update-slice), channel_id=2, replica_groups=mesh['al'=32,'ka'=16] {'al'}, use_global_device_ids=true, to_apply=%add.2 | all-reduce | flops 32 | bytes 256
  22.4 43.0 %while.13 = (s32[]{:T(128)}, s32[1]{0:T(128)}, s32[]{:T(128)}, s32[32,1]{0,1:T(1,128)S(1)}, s32[]{:T(128)}) while((s32[]{:T(128)}, s32[1]{0:T(128)}, s32[]{:T(128)}, s32[32,1]{0,1:T(1,128)S(1)}, s32[]{:T(128)}) %tuple.69), condition=%wide.region_1.2_spmd, body=%wide.region_0.1_spmd.sunk | while | flops 5 | bytes 115 | solution.py:19
  25.2 0.7 constant_dynamic-slice_fusion.2
  26.6 0.7 constant_dynamic-slice_fusion.2
  28.0 0.7 constant_dynamic-slice_fusion.2
  29.4 0.7 constant_dynamic-slice_fusion.2
  32.1 0.7 constant_dynamic-slice_fusion.2
  34.9 0.7 constant_dynamic-slice_fusion.2
  36.3 0.7 constant_dynamic-slice_fusion.2
  37.7 0.7 constant_dynamic-slice_fusion.2
  39.1 0.7 constant_dynamic-slice_fusion.2
  41.8 0.7 constant_dynamic-slice_fusion.2
  43.2 0.7 constant_dynamic-slice_fusion.2
  44.6 0.7 constant_dynamic-slice_fusion.2
  46.0 0.7 constant_dynamic-slice_fusion.2
  47.4 0.7 constant_dynamic-slice_fusion.2
  48.8 0.7 constant_dynamic-slice_fusion.2
  51.6 0.7 constant_dynamic-slice_fusion.2
  52.9 0.7 constant_dynamic-slice_fusion.2
  54.3 0.7 constant_dynamic-slice_fusion.2
  55.7 0.7 constant_dynamic-slice_fusion.2
  58.5 0.7 constant_dynamic-slice_fusion.2
  61.3 0.7 constant_dynamic-slice_fusion.2
  65.5 0.9 select_reduce_fusion.1
  66.4 1.7 fusion.101
  68.2 2.1 %collective-permute-start = (bf16[128,128]{1,0:T(8,128)(2,1)S(1)}, bf16[128,128]{1,0:T(8,128)(2,1)S(1)}, u32[]{:S(2)}, u32[]{:S(2)}) collective-permute-start(bf16[128,128]{1,0:T(8,128)(2,1)S(1)} %fusion.69), channel_id=1, source_target_pairs={{0,16},{16,32},{32,48},{48,64},{64,80},{80,96},{96,112},{112,128},... | collective-permute-start | bytes 98312 | tf_op jit(solution)/shard_map/ppermute | solution.py:33
  70.3 0.8 slice_bitcast_fusion.1
  71.0 5.3 %collective-permute-start.1 = (bf16[128,128]{1,0:T(8,128)(2,1)S(1)}, bf16[128,128]{1,0:T(8,128)(2,1)S(1)}, u32[]{:S(2)}, u32[]{:S(2)}) collective-permute-start(bf16[128,128]{1,0:T(8,128)(2,1)S(1)} %slice_bitcast_fusion.1), channel_id=1, source_target_pairs={{16,0},{32,16},{48,32},{64,48},{80,64},{96,80},{112,96},{128,112},... | collective-permute-start | bytes 98312 | tf_op jit(solution)/shard_map/ppermute | solution.py:33
  76.4 1.4 fusion.106
  81.1 1.1 fusion.59
  82.2 1.0 fusion.64
  83.2 0.7 fusion.24
  83.9 35.3 %all-gather.4.cloned.1.call-done = bf16[4,2048,128]{2,1,0:T(8,128)(2,1)} async-done(((bf16[4,128,128]{2,1,0:T(8,128)(2,1)}), bf16[4,2048,128]{2,1,0:T(8,128)(2,1)}) %all-gather.4.cloned.1.call-update) | async-done | bytes 2097168 | tf_op jit(solution)/shard_map/all_gather | solution.py:115
  119.1 3.2 %convert_bitcast_fusion.1 = bf16[4,16,128,128]{2,3,1,0:T(8,128)(2,1)S(1)} fusion(bf16[4,16,128,128]{3,2,1,0:T(8,128)(2,1)} %bitcast.56, bf16[4,128,2048]{2,1,0:T(8,128)(2,1)S(1)} %copy-done), kind=kOutput, calls=%fused_computation.8 | convolution fusion | flops 269484032 | bytes 6291456 | tf_op jit(solution)/shard_map/jrbk,jbkn->jbrn/dot_general | solution.py:118
  122.8 1.8 %fusion.12 = f32[4,128,128]{2,1,0:T(8,128)S(1)} fusion(f32[4,128,128]{2,1,0:T(8,128)S(1)} %fusion.24, f32[3,128,128]{2,1,0:T(8,128)S(1)} %get-tuple-element.106, f32[1,128,128]{2,1,0:T(8,128)S(1)} %bitcast_convert_fusion.1, f32[4,64,64]{1,2,0:T(8,128)} %get-tuple-element.112, f32[4,64,64]{1,2,0:T(8,128)} %get-tuple-element.109, ...), kind=kOutput, calls=%fused_computation.15 | convolution fusion | flops 101253120 | bytes 1508352 | tf_op jit(solution)/shard_map/jrn,jnp->jrp/dot_general | solution.py:140
  124.9 0.8 fusion.99
  125.7 0.8 slice_bitcast_fusion
  126.5 5.2 %collective-permute-start.3 = (bf16[128,128]{1,0:T(8,128)(2,1)S(1)}, bf16[128,128]{1,0:T(8,128)(2,1)S(1)}, u32[]{:S(2)}, u32[]{:S(2)}) collective-permute-start(bf16[128,128]{1,0:T(8,128)(2,1)S(1)} %slice_bitcast_fusion), channel_id=1, source_target_pairs={{16,0},{32,16},{48,32},{64,48},{80,64},{96,80},{112,96},{128,112},... | collective-permute-start | bytes 98312 | tf_op jit(solution)/shard_map/ppermute | solution.py:33
  131.7 1.9 %collective-permute-start.2 = (bf16[128,128]{1,0:T(8,128)(2,1)S(1)}, bf16[128,128]{1,0:T(8,128)(2,1)S(1)}, u32[]{:S(2)}, u32[]{:S(2)}) collective-permute-start(bf16[128,128]{1,0:T(8,128)(2,1)S(1)} %fusion.70), channel_id=1, source_target_pairs={{0,16},{16,32},{32,48},{48,64},{64,80},{80,96},{96,112},{112,128},... | collective-permute-start | bytes 98312 | tf_op jit(solution)/shard_map/ppermute | solution.py:33
  133.6 0.7 fusion.103
  134.3 4.1 %collective-permute-done.2 = bf16[128,128]{1,0:T(8,128)(2,1)S(1)} collective-permute-done((bf16[128,128]{1,0:T(8,128)(2,1)S(1)}, bf16[128,128]{1,0:T(8,128)(2,1)S(1)}, u32[]{:S(2)}, u32[]{:S(2)}) %collective-permute-start.2) | collective-permute-done | bytes 32800 | tf_op jit(solution)/shard_map/ppermute | solution.py:33
  139.1 0.7 fusion.43
  139.8 27.3 %all-gather.6.cloned.1.call-done = bf16[4,2048,128]{2,1,0:T(8,128)(2,1)} async-done(((bf16[4,128,128]{2,1,0:T(8,128)(2,1)}), bf16[4,2048,128]{2,1,0:T(8,128)(2,1)}) %all-gather.6.cloned.1.call-update) | async-done | bytes 2097168 | tf_op jit(solution)/shard_map/all_gather | solution.py:115
  167.1 3.2 %convert_bitcast_fusion = bf16[4,16,128,128]{2,3,1,0:T(8,128)(2,1)S(1)} fusion(bf16[4,16,128,128]{3,2,1,0:T(8,128)(2,1)} %bitcast.57, bf16[4,128,2048]{2,1,0:T(8,128)(2,1)S(1)} %copy-done), kind=kOutput, calls=%fused_computation.7 | convolution fusion | flops 269484032 | bytes 6291456 | tf_op jit(solution)/shard_map/jrbk,jbkn->jbrn/dot_general | solution.py:118
  170.8 1.9 %fusion.13 = f32[4,128,128]{2,1,0:T(8,128)S(1)} fusion(f32[4,128,128]{2,1,0:T(8,128)S(1)} %fusion.43, f32[3,128,128]{2,1,0:T(8,128)} %get-tuple-element.102, f32[1,128,128]{2,1,0:T(8,128)} %bitcast_convert_fusion, f32[4,64,64]{1,2,0:T(8,128)} %get-tuple-element.111, f32[4,64,64]{1,2,0:T(8,128)} %get-tuple-element.113, ...), kind=kOutput, calls=%fused_computation.16 | convolution fusion | flops 101253120 | bytes 1508352 | tf_op jit(solution)/shard_map/jrn,jnp->jrp/dot_general | solution.py:140
  172.9 0.9 fusion.52
  (64 shorter events, 9.5 us)
Async XLA Ops:
  6.5 112.6 %copy-start = (bf16[4,128,2048]{2,1,0:T(8,128)(2,1)S(1)}, bf16[4,128,2048]{2,1,0:T(8,128)(2,1)}, u32[]{:S(2)}) copy-start(bf16[4,128,2048]{2,1,0:T(8,128)(2,1)} %param.8) | copy-start | bytes 6291460
  6.5 112.6 %all-gather.4.cloned.1.call-start = ((), (), s32[]{:S(2)}) async-start(), calls=%async_computation | async-start | bytes 2228224 | tf_op jit(solution)/shard_map/all_gather | solution.py:115
  68.1 99.1 %all-gather.6.cloned.1.call-start = ((), (), s32[]{:S(2)}) async-start(), calls=%async_computation.1 | async-start | bytes 2228224 | tf_op jit(solution)/shard_map/all_gather | solution.py:115
  68.2 15.0 %collective-permute-start = (bf16[128,128]{1,0:T(8,128)(2,1)S(1)}, bf16[128,128]{1,0:T(8,128)(2,1)S(1)}, u32[]{:S(2)}, u32[]{:S(2)}) collective-permute-start(bf16[128,128]{1,0:T(8,128)(2,1)S(1)} %fusion.69), channel_id=1, source_target_pairs={{0,16},{16,32},{32,48},{48,64},{64,80},{80,96},{96,112},{112,128},... | collective-permute-start | bytes 98312 | tf_op jit(solution)/shard_map/ppermute | solution.py:33
  71.0 12.1 %collective-permute-start.1 = (bf16[128,128]{1,0:T(8,128)(2,1)S(1)}, bf16[128,128]{1,0:T(8,128)(2,1)S(1)}, u32[]{:S(2)}, u32[]{:S(2)}) collective-permute-start(bf16[128,128]{1,0:T(8,128)(2,1)S(1)} %slice_bitcast_fusion.1), channel_id=1, source_target_pairs={{16,0},{32,16},{48,32},{64,48},{80,64},{96,80},{112,96},{128,112},... | collective-permute-start | bytes 98312 | tf_op jit(solution)/shard_map/ppermute | solution.py:33
  124.7 14.4 %copy-start.1 = (f32[4,64,64]{1,2,0:T(8,128)S(1)}, f32[4,64,64]{1,2,0:T(8,128)}, u32[]{:S(2)}) copy-start(f32[4,64,64]{1,2,0:T(8,128)} %get-tuple-element.115) | copy-start | bytes 196612
  124.7 14.4 %copy-start.2 = (f32[4,64,64]{1,2,0:T(8,128)S(1)}, f32[4,64,64]{1,2,0:T(8,128)}, u32[]{:S(2)}) copy-start(f32[4,64,64]{1,2,0:T(8,128)} %get-tuple-element.117) | copy-start | bytes 196612
  124.7 14.4 %copy-start.3 = (f32[4,64,64]{1,2,0:T(8,128)S(1)}, f32[4,64,64]{1,2,0:T(8,128)}, u32[]{:S(2)}) copy-start(f32[4,64,64]{1,2,0:T(8,128)} %get-tuple-element.118) | copy-start | bytes 196612
  126.5 7.8 %collective-permute-start.3 = (bf16[128,128]{1,0:T(8,128)(2,1)S(1)}, bf16[128,128]{1,0:T(8,128)(2,1)S(1)}, u32[]{:S(2)}, u32[]{:S(2)}) collective-permute-start(bf16[128,128]{1,0:T(8,128)(2,1)S(1)} %slice_bitcast_fusion), channel_id=1, source_target_pairs={{16,0},{32,16},{48,32},{64,48},{80,64},{96,80},{112,96},{128,112},... | collective-permute-start | bytes 98312 | tf_op jit(solution)/shard_map/ppermute | solution.py:33
  131.7 6.8 %collective-permute-start.2 = (bf16[128,128]{1,0:T(8,128)(2,1)S(1)}, bf16[128,128]{1,0:T(8,128)(2,1)S(1)}, u32[]{:S(2)}, u32[]{:S(2)}) collective-permute-start(bf16[128,128]{1,0:T(8,128)(2,1)S(1)} %fusion.70), channel_id=1, source_target_pairs={{0,16},{16,32},{32,48},{48,64},{64,80},{80,96},{96,112},{112,128},... | collective-permute-start | bytes 98312 | tf_op jit(solution)/shard_map/ppermute | solution.py:33
Sparse Core Ops, SparseCore 0:
  68.2 50.8 all-gather.3
  125.8 41.2 all-gather.5
where the time goes:
time: 183 us; the launch traced here: 181 us
  waiting for transfers between devices  66.8 us (37%)
  local copies, waits for them, and re-layouts  26.8 us (15%)
  loops' own time  22.3 us (12%)
  between operations  17 us (9%)
  starting transfers between devices  14.5 us (8%)
  blocking collectives  12.9 us (7%)
  matrix products  11.6 us (6%)
  other arithmetic  8.67 us (5%)
    all_gather x2, waiting for transfers between devices, kernel_apply(): gathered = lax.all_gather(rounded, 'ka', axis=1, tiled=True)  62.6 us
    another operation x1, loops' own time, entering(): return lax.fori_loop(0, count - 1, turn, total)  22.3 us
    dynamic_slice x31, local copies, waits for them, and re-layouts, turn(): longer = join(total, pieces[position])  20.7 us
    ppermute x4, starting transfers between devices, passed_along(): return lax.ppermute(block, axis, route)  14.5 us
    unnamed x1, blocking collectives  12.9 us
    dot_general x2, matrix products, kernel_apply(): jnp.einsum('jrbk,jbkn->jbrn', kernel_blocks, state_blocks, preferred_elem...  6.39 us
    ppermute x4, waiting for transfers between devices, passed_along(): return lax.ppermute(block, axis, route)  4.13 us
    dot_general x2, matrix products, time_derivative(): jnp.einsum('jrn,jnp->jrp', below_state, lower_mix, precision=lax.Precisio...  3.76 us
  transfers between devices with their start and end apart: 6, of which 3 were waited for; matrix products, arithmetic and copies ran while one was open for 5% of the time, Pallas kernels for 0%

commit v1 on v0

v1 whole, which is shorter than its diff:
```python
import functools

import jax
import jax.numpy as jnp
from jax import lax
from jax.experimental import pallas as pl
from jax.experimental.pallas import tpu as pltpu
from jax.sharding import PartitionSpec as P

step_length = 0.2
momentum_top = 3.0
TOP = 13
VMEM_LIMIT = 32 * 1024 * 1024


def encode(rounded, out_ref, slot):
    rows, lanes = rounded.shape
    values = rounded.astype(jnp.float32)
    largest = jnp.max(jnp.abs(values), axis=0, keepdims=True)
    exponent = jnp.clip(jnp.floor(jnp.log2(jnp.maximum(largest, 1e-36))), -110.0, 127.0)
    scaled = values * jnp.exp2(TOP - exponent)
    out_ref[slot * rows : (slot + 1) * rows, :] = scaled.astype(out_ref.dtype)
    return exponent


def store_exponents(exponents, out_ref, start):
    lanes = exponents[0].shape[1]
    pad = out_ref.shape[0] - start - len(exponents)
    rows = jnp.concatenate(exponents + [jnp.zeros((pad, lanes), jnp.float32)], axis=0)
    out_ref[start:, :] = rows.astype(out_ref.dtype)


def encode_kernel(slots, held_ref, psi_ref, out_ref, low_ref, high_ref):
    rows = psi_ref.shape[1]
    exponents = []
    for slot in range(slots):
        rounded = psi_ref[slot].astype(jnp.bfloat16)
        exponents.append(encode(rounded, out_ref, slot))
    store_exponents(exponents, out_ref, slots * rows)
    low_ref[...] = psi_ref[0].astype(jnp.bfloat16)
    high_ref[...] = psi_ref[held_ref[0] - 1].astype(jnp.bfloat16)


def kernel_product(slot, slots, rows, blocks, gathered_ref, kernel_ref, scales):
    total = None
    for pair in range(0, blocks, 2):
        pieces = []
        for block in (pair, pair + 1):
            piece = gathered_ref[block, slot * rows : (slot + 1) * rows, :]
            scale = scales[block][slot : slot + 1]
            pieces.append((piece.astype(jnp.float32) * scale).astype(jnp.bfloat16))
        part = jnp.dot(
            kernel_ref[slot, :, pair * rows : (pair + 2) * rows],
            jnp.concatenate(pieces, axis=0),
            preferred_element_type=jnp.float32,
        )
        total = part if total is None else total + part
    return total


def read_scales(slots, rows, blocks, gathered_ref):
    start = slots * rows
    return [
        jnp.exp2(gathered_ref[b, start : start + 16, :].astype(jnp.float32) - TOP)
        for b in range(blocks)
    ]


def raise_to(v, n):
    return jnp.sqrt(
        jnp.maximum((v + n + 1.0) * (v + n + 2.0) / jnp.maximum((2.0 * v + 1.0) * (2.0 * v + 3.0), 1.0), 0.0)
    )


def drop_to(v, n):
    return -jnp.sqrt(
        jnp.maximum((v - n) * (v - n - 1.0), 0.0) / jnp.maximum((2.0 * v - 1.0) * (2.0 * v + 1.0), 1.0)
    )


def derivative(
    slot, first, held, waves, counts_ref, field_x, field_y, momenta, current, kernel_term, below, above
):
    rows, lanes = current.shape
    mslots = lanes // 2
    wave = first + slot
    low, high = wave - 1, wave + 1

    def count_of(index):
        return counts_ref[jnp.clip(index, 0, waves - 1)]

    count, count_low, count_high = count_of(wave), count_of(low), count_of(high)
    lane = lax.broadcasted_iota(jnp.int32, (1, lanes), 1)
    q = jnp.where(lane < mslots, lane, lane - mslots)
    m = (q - (count - 1) // 2).astype(jnp.float32)
    wave_f = wave.astype(jnp.float32)
    inside = q < count

    def moved(source, count_source, present, change, factor):
        shift = (count_source - 1) // 2 - (count - 1) // 2 - change
        p = q + shift
        allowed = inside & (p >= 0) & (p < count_source) & present
        turned = pltpu.roll(source, lax.rem(2 * lanes - shift, lanes), 1)
        return jnp.where(allowed, factor, 0.0) * turned

    has_low, has_high = low >= 0, high < waves
    up = moved(below, count_low, has_low, 1, raise_to(wave_f - 1.0, m - 1.0))
    up = up + moved(above, count_high, has_high, 1, drop_to(wave_f + 1.0, m - 1.0))
    down = moved(below, count_low, has_low, -1, drop_to(wave_f, m))
    down = down + moved(above, count_high, has_high, -1, raise_to(wave_f, m))
    turn = 0.5 * (momenta * momenta) * current + kernel_term + momenta * ((0.5 * field_x) * (up + down))
    swapped = pltpu.roll(turn, mslots, 1)
    swapped = jnp.where(lane < mslots, swapped, -swapped)
    flow = swapped + momenta * ((0.5 * field_y) * (down - up))
    return flow, inside & (slot < held)


def keep_of(slot, first, held, waves, counts_ref, lanes):
    count = counts_ref[jnp.clip(first + slot, 0, waves - 1)]
    lane = lax.broadcasted_iota(jnp.int32, (1, lanes), 1)
    q = jnp.where(lane < lanes // 2, lane, lane - lanes // 2)
    return (q < count) & (slot < held)


def momenta_of(place, rows, radial_count):
    row = lax.broadcasted_iota(jnp.int32, (rows, 1), 0) + place * rows
    return (row.astype(jnp.float32) + 0.5) * (momentum_top / radial_count)


def half_kernel(
    slots, waves, blocks, al_count,
    place_ref, held_ref, counts_ref, field_ref, psi_ref, gathered_ref, kernel_ref, below_ref, above_ref,
    half_ref, out_ref, low_ref, high_ref, first_ref,
):
    rows, lanes = psi_ref.shape[1:]
    al, ka = place_ref[0], place_ref[1]
    held = held_ref[0]
    start = slots * rows
    seen = None
    for block in range(blocks):
        row = gathered_ref[block, start : start + 16, :].astype(jnp.float32)[8:9]
        seen = row if seen is None else seen + row
    seen = jnp.max(seen).astype(jnp.int32)
    first = jnp.where(2 * al < al_count, seen, waves - held - seen)
    first_ref[0] = first
    momenta = momenta_of(ka, rows, kernel_ref.shape[2])
    scales = read_scales(slots, rows, blocks, gathered_ref)
    psi = [
        jnp.where(keep_of(s, first, held, waves, counts_ref, lanes), psi_ref[s], 0.0) for s in range(slots)
    ]
    lowest, highest = below_ref[...].astype(jnp.float32), above_ref[...].astype(jnp.float32)
    exponents = []
    for slot in range(slots):
        term = kernel_product(slot, slots, rows, blocks, gathered_ref, kernel_ref, scales)
        below = lowest if slot == 0 else psi[slot - 1]
        above = highest if slot == slots - 1 else jnp.where(slot + 1 < held, psi[slot + 1], highest)
        flow, keep = derivative(
            slot, first, held, waves, counts_ref, field_ref[0, 0], field_ref[0, 1], momenta,
            psi[slot], term, below, above,
        )
        half = jnp.where(keep, psi[slot] + (0.5 * step_length) * flow, 0.0)
        half_ref[slot] = half
        rounded = half.astype(jnp.bfloat16)
        exponents.append(encode(rounded, out_ref, slot))
        if slot == 0:
            low_ref[...] = rounded

        @pl.when(slot == held - 1)
        def _():
            high_ref[...] = rounded

    store_exponents(exponents, out_ref, start)


def product_kernel(slots, blocks, gathered_ref, kernel_ref, out_ref):
    rows = out_ref.shape[1]
    scales = read_scales(slots, rows, blocks, gathered_ref)
    for slot in range(slots):
        out_ref[slot] = kernel_product(slot, slots, rows, blocks, gathered_ref, kernel_ref, scales)


def last_kernel(
    slots, waves, radial_count,
    place_ref, held_ref, first_ref, counts_ref, field_ref, psi_ref, half_ref, term_ref, below_ref, above_ref,
    out_ref,
):
    rows, lanes = psi_ref.shape[1:]
    held, first = held_ref[0], first_ref[0]
    momenta = momenta_of(place_ref[1], rows, radial_count)
    lowest, highest = below_ref[...].astype(jnp.float32), above_ref[...].astype(jnp.float32)
    for slot in range(slots):
        below = lowest if slot == 0 else half_ref[slot - 1]
        above = highest if slot == slots - 1 else jnp.where(slot + 1 < held, half_ref[slot + 1], highest)
        flow, keep = derivative(
            slot, first, held, waves, counts_ref, field_ref[1, 0], field_ref[1, 1], momenta,
            half_ref[slot], term_ref[slot], below, above,
        )
        out_ref[slot] = jnp.where(keep, psi_ref[slot] + step_length * flow, 0.0)


def shards(al_count, ka_count, amplitudes, kernel, block_lengths, m_counts, vector_potential):
    slots, rows, lanes = amplitudes.shape
    radial_count = kernel.shape[2]
    waves = m_counts.shape[0]
    sent_rows = slots * rows + 16
    smem = pl.BlockSpec(memory_space=pltpu.SMEM)
    vmem = pl.BlockSpec(memory_space=pltpu.VMEM)
    params = pltpu.CompilerParams(vmem_limit_bytes=VMEM_LIMIT)
    f32, bf16 = jnp.float32, jnp.bfloat16
    shape = jax.ShapeDtypeStruct
    edge = shape((rows, lanes), bf16)
    sent = shape((sent_rows, lanes), bf16)
    state = shape((slots, rows, lanes), f32)
    place = jnp.stack([lax.axis_index("al"), lax.axis_index("ka")]).astype(jnp.int32)

    route = []
    for d in range(al_count):
        for k in range(1, ka_count):
            source = d - k if 2 * d < al_count else d + k
            if 0 <= source < al_count:
                route.append((source * ka_count + k, d * ka_count + k))
    other = lax.ppermute(block_lengths, ("al", "ka"), route)
    upward = [(i, i + 1) for i in range(al_count - 1)]
    downward = [(i + 1, i) for i in range(al_count - 1)]

    def exchange(low, high):
        return lax.ppermute(high, "al", upward), lax.ppermute(low, "al", downward)

    def gather(payload):
        payload = lax.optimization_barrier(payload.astype(jnp.float16))
        everything = lax.optimization_barrier(lax.all_gather(payload, "ka", axis=0, tiled=False))
        return everything.astype(bf16)

    encoded, low, high = pl.pallas_call(
        functools.partial(encode_kernel, slots),
        out_shape=(sent, edge, edge),
        in_specs=[smem, vmem],
        out_specs=(vmem, vmem, vmem),
        compiler_params=params,
        name="encode",
    )(block_lengths, amplitudes)
    below, above = exchange(low, high)
    row = lax.broadcasted_iota(jnp.int32, (sent_rows, lanes), 0)
    encoded = jnp.where(row >= sent_rows - 8, other[0].astype(f32).astype(bf16), encoded)
    gathered = gather(encoded)
    half, encoded, low, high, first = pl.pallas_call(
        functools.partial(half_kernel, slots, waves, ka_count, al_count),
        out_shape=(state, sent, edge, edge, shape((1,), jnp.int32)),
        in_specs=[smem] * 4 + [vmem] * 5,
        out_specs=(vmem, vmem, vmem, vmem, smem),
        compiler_params=params,
        name="half",
    )(place, block_lengths, m_counts, vector_potential, amplitudes, gathered, kernel, below, above)
    gathered = gather(encoded)
    below, above = exchange(low, high)
    term = pl.pallas_call(
        functools.partial(product_kernel, slots, ka_count),
        out_shape=state,
        in_specs=[vmem] * 2,
        out_specs=vmem,
        compiler_params=params,
        cost_estimate=pl.CostEstimate(
            flops=2 * slots * rows * radial_count * lanes * 8, bytes_accessed=4 * 1024 * 1024, transcendentals=0
        ),
        name="product",
    )(gathered, kernel)
    return pl.pallas_call(
        functools.partial(last_kernel, slots, waves, radial_count),
        out_shape=state,
        in_specs=[smem] * 5 + [vmem] * 5,
        out_specs=vmem,
        compiler_params=params,
        name="last",
    )(place, block_lengths, first, m_counts, vector_potential, amplitudes, half, term, below, above)


def solution(mesh):
    in_specs = (P("al", "ka", None), P("al", "ka", None), P("al"), P(), P())
    out_specs = P("al", "ka", None)
    body = functools.partial(shards, mesh.shape["al"], mesh.shape["ka"])
    return jax.shard_map(body, mesh=mesh, in_specs=in_specs, out_specs=out_specs, check_vma=False)
```

time: 183 us -> 85.2 us (0.47); the launches traced: 181 us -> 84.8 us
  waiting for transfers between devices: 66.8 us -> 0.01 us
  blocking collectives: 12.9 us -> 54 us
  local copies, waits for them, and re-layouts: 26.8 us -> 2.23 us
  loops' own time: 22.3 us -> 0 us
  between operations: 17 us -> 1.45 us
  matrix products: 11.6 us -> 0 us
  other arithmetic: 8.67 us -> 1 us
  Pallas kernels: 0 us -> 6.22 us
  starting transfers between devices: 14.5 us -> 19.9 us
    all_gather x2 -> x0, waiting for transfers between devices: 62.6 us -> none  [kernel_apply(): gathered = lax.all_gather(rounded, 'ka', axis=1, tiled=True)]
    all_gather x0 -> x2, blocking collectives: none -> 54 us  [gather(): lax.all_gather(payload, 'ka', axis=0, tiled=False)]
    another operation x1 -> x0, loops' own time: 22.3 us -> none  [entering(): return lax.fori_loop(0, count - 1, turn, total)]
    dynamic_slice x31 -> x0, local copies, waits for them, and re-layouts: 20.7 us -> none  [turn(): longer = join(total, pieces[position])]
    unnamed x1 -> x0, blocking collectives: 12.9 us -> none
    dot_general x6 -> x0, matrix products: 11.6 us -> none  [the longest x2 6.39 us: kernel_apply(): jnp.einsum('jrbk,jbkn->jbrn', kernel_blocks, state_blocks, preferred_elem...]
    pallas_call x0 -> x4, Pallas kernels: none -> 6.22 us  [the longest x1 2.79 us: shards(): pl.pallas_call(functools.partial(half_kernel, slots, waves, ka_count, al_...]
    ppermute x4 -> x5, starting transfers between devices: 14.5 us -> 19.9 us  [the longest x4 14.8 us: exchange(): return (lax.ppermute(high, 'al', upward), lax.ppermute(low, 'al', downward))]
  transfers between devices with their start and end apart: 6 -> 5, of which waited for: 3 -> 0; matrix products, arithmetic and copies ran while one was open for 5% -> 1% of each run, Pallas kernels for 0% -> 1%
where the time goes in v1:
time: 85.2 us; the launch traced here: 84.8 us
  blocking collectives  54 us (63%)
  starting transfers between devices  19.9 us (23%)
  Pallas kernels  6.22 us (7%)
  local copies, waits for them, and re-layouts  2.23 us (3%)
  between operations  1.45 us (2%)
  other arithmetic  1 us (1%)
    all_gather x2, blocking collectives, gather(): lax.all_gather(payload, 'ka', axis=0, tiled=False)  54 us
    ppermute x4, starting transfers between devices, exchange(): return (lax.ppermute(high, 'al', upward), lax.ppermute(low, 'al', downward))  14.8 us
    ppermute x1, starting transfers between devices, shards(): other = lax.ppermute(block_lengths, ('al', 'ka'), route)  5.16 us
    pallas_call x1, Pallas kernels, shards(): pl.pallas_call(functools.partial(half_kernel, slots, waves, ka_count, al_...  2.79 us
    pallas_call x1, Pallas kernels, shards(): pl.pallas_call(functools.partial(last_kernel, slots, waves, radial_count)...  2.53 us
    unnamed x10, local copies, waits for them, and re-layouts  2.23 us
  transfers between devices with their start and end apart: 5, of which 0 were waited for; matrix products, arithmetic and copies ran while one was open for 1% of the time, Pallas kernels for 1%

profile of v1, /device:TPU:57, one launch (start us, length us, event | category | flops | bytes accessed | tf_op | source)
XLA Modules:
  0.0 84.8 jit_solution(4204266144972539512)
XLA Ops:
  0.0 5.2 %collective-permute-start = (s32[1]{0:T(128)}, s32[1]{0:T(128)}, u32[]{:S(2)}, u32[]{:S(2)}) collective-permute-start(s32[1]{0:T(128)} %param.7), channel_id=1, source_target_pairs={{1,17},{17,33},{2,34},{33,49},{18,50},{3,51},{49,65},{34,66},{19,6... | collective-permute-start | bytes 20 | tf_op jit(solution)/shard_map/ppermute | solution.py:222
  5.8 0.0 copy-start
  5.8 0.9 %copy-done = f32[4,128,128]{2,1,0:T(8,128)S(1)} copy-done((f32[4,128,128]{2,1,0:T(8,128)S(1)}, f32[4,128,128]{2,1,0:T(8,128)}, u32[]{:S(2)}) %copy-start) | copy-done | bytes 262168
  6.8 0.1 encode.1
  6.9 1.9 %collective-permute-start.1 = (bf16[128,128]{1,0:T(8,128)(2,1)S(1)}, bf16[128,128]{1,0:T(8,128)(2,1)S(1)}, u32[]{:S(2)}, u32[]{:S(2)}) collective-permute-start(bf16[128,128]{1,0:T(8,128)(2,1)S(1)} %get-tuple-element.14), channel_id=1, source_target_pairs={{0,16},{16,32},{32,48},{48,64},{64,80},{80,96},{96,112},{112,128},... | collective-permute-start | bytes 98312 | tf_op jit(solution)/shard_map/ppermute | solution.py:227
  8.8 5.5 %collective-permute-start.2 = (bf16[128,128]{1,0:T(8,128)(2,1)S(1)}, bf16[128,128]{1,0:T(8,128)(2,1)S(1)}, u32[]{:S(2)}, u32[]{:S(2)}) collective-permute-start(bf16[128,128]{1,0:T(8,128)(2,1)S(1)} %get-tuple-element.15), channel_id=1, source_target_pairs={{16,0},{32,16},{48,32},{64,48},{80,64},{96,80},{112,96},{128,112},... | collective-permute-start | bytes 98312 | tf_op jit(solution)/shard_map/ppermute | solution.py:227
  14.3 0.1 pad_add_fusion.place_ref
  14.4 0.0 collective-permute-done
  15.0 0.1 select_convert_fusion
  15.1 30.7 %all-gather.4 = f16[8448,128]{1,0:T(8,128)(2,1)S(1)} all-gather(f16[528,128]{1,0:T(8,128)(2,1)S(1)} %select_convert_fusion), channel_id=2, replica_groups=mesh['al'=32,'ka'=16] {'ka'}, dimensions={0}, use_global_device_ids=true | all-gather | bytes 2297856 | tf_op jit(solution)/shard_map/all_gather | solution.py:231
  45.9 0.0 copy-start.1
  45.9 0.0 copy-start.2
  45.9 0.0 copy-start.3
  45.9 0.0 copy-start.4
  45.9 0.4 convert_element_type.26.gathered_ref
  46.3 0.0 collective-permute-done.1.below_ref
  46.3 0.0 collective-permute-done.2.above_ref
  46.3 0.5 copy-done.1
  46.8 0.7 copy-done.2
  47.6 0.0 copy-done.3
  47.6 0.0 copy-done.4
  47.6 2.8 %half.1 = (f32[4,128,128]{2,1,0:T(8,128)S(1)}, bf16[528,128]{1,0:T(8,128)(2,1)S(1)}, bf16[128,128]{1,0:T(8,128)(2,1)S(1)}, bf16[128,128]{1,0:T(8,128)(2,1)S(1)}, s32[1]{0:T(128)}) custom-call(s32[2]{0:T(128)S(1)} %pad_add_fusion.place_ref, s32[1]{0:T(128)S(6)} %copy.6.held_ref, s32[64]{0:T(128)S(1)} %copy-done.4, f32[2,2]{1,0:T(2,128)S(1)} %copy-done.3, ...), custom_call_target="tpu_custom_call" | custom-call | tf_op jit(solution)/shard_map/half/pallas_call | solution.py:246
  50.4 1.9 %collective-permute-start.3 = (bf16[128,128]{1,0:T(8,128)(2,1)S(1)}, bf16[128,128]{1,0:T(8,128)(2,1)S(1)}, u32[]{:S(2)}, u32[]{:S(2)}) collective-permute-start(bf16[128,128]{1,0:T(8,128)(2,1)S(1)} %get-tuple-element.19), channel_id=1, source_target_pairs={{0,16},{16,32},{32,48},{48,64},{64,80},{80,96},{96,112},{112,128},... | collective-permute-start | bytes 98312 | tf_op jit(solution)/shard_map/ppermute | solution.py:227
  52.3 5.5 %collective-permute-start.4 = (bf16[128,128]{1,0:T(8,128)(2,1)S(1)}, bf16[128,128]{1,0:T(8,128)(2,1)S(1)}, u32[]{:S(2)}, u32[]{:S(2)}) collective-permute-start(bf16[128,128]{1,0:T(8,128)(2,1)S(1)} %get-tuple-element.20), channel_id=1, source_target_pairs={{16,0},{32,16},{48,32},{64,48},{80,64},{96,80},{112,96},{128,112},... | collective-permute-start | bytes 98312 | tf_op jit(solution)/shard_map/ppermute | solution.py:227
  57.8 23.3 %all-gather.5 = f16[8448,128]{1,0:T(8,128)(2,1)S(1)} all-gather(f16[528,128]{1,0:T(8,128)(2,1)S(1)} %convert_element_type.27), channel_id=3, replica_groups=mesh['al'=32,'ka'=16] {'ka'}, dimensions={0}, use_global_device_ids=true | all-gather | bytes 2297856 | tf_op jit(solution)/shard_map/all_gather | solution.py:231
  81.1 0.4 convert_element_type.28.gathered_ref
  81.4 0.8 product.1.term_ref
  82.3 0.0 collective-permute-done.3.below_ref
  82.3 0.0 collective-permute-done.4.above_ref
  82.3 2.5 %last.1 = f32[4,128,128]{2,1,0:T(8,128)} custom-call(s32[2]{0:T(128)S(1)} %pad_add_fusion.place_ref, s32[1]{0:T(128)S(6)} %copy.6.held_ref, s32[1]{0:T(128)} %get-tuple-element.16.first_ref, s32[64]{0:T(128)S(1)} %copy-done.4, f32[2,2]{1,0:T(2,128)S(1)} %copy-done.3, f32[4,128,128]{2,1,0:T(8,128)S(1)} %copy-done.1, ...), custom_call_target="tpu_custom_call" | custom-call | tf_op jit(solution)/shard_map/last/pallas_call | solution.py:267
  (2 shorter events, 0.0 us)
Async XLA Ops:
  0.0 14.4 %collective-permute-start = (s32[1]{0:T(128)}, s32[1]{0:T(128)}, u32[]{:S(2)}, u32[]{:S(2)}) collective-permute-start(s32[1]{0:T(128)} %param.7), channel_id=1, source_target_pairs={{1,17},{17,33},{2,34},{33,49},{18,50},{3,51},{49,65},{34,66},{19,6... | collective-permute-start | bytes 20 | tf_op jit(solution)/shard_map/ppermute | solution.py:222
  5.8 1.0 %copy-start = (f32[4,128,128]{2,1,0:T(8,128)S(1)}, f32[4,128,128]{2,1,0:T(8,128)}, u32[]{:S(2)}) copy-start(f32[4,128,128]{2,1,0:T(8,128)} %psi_ref.5) | copy-start | bytes 786436
  6.9 39.4 %collective-permute-start.1 = (bf16[128,128]{1,0:T(8,128)(2,1)S(1)}, bf16[128,128]{1,0:T(8,128)(2,1)S(1)}, u32[]{:S(2)}, u32[]{:S(2)}) collective-permute-start(bf16[128,128]{1,0:T(8,128)(2,1)S(1)} %get-tuple-element.14), channel_id=1, source_target_pairs={{0,16},{16,32},{32,48},{48,64},{64,80},{80,96},{96,112},{112,128},... | collective-permute-start | bytes 98312 | tf_op jit(solution)/shard_map/ppermute | solution.py:227
  8.8 37.5 %collective-permute-start.2 = (bf16[128,128]{1,0:T(8,128)(2,1)S(1)}, bf16[128,128]{1,0:T(8,128)(2,1)S(1)}, u32[]{:S(2)}, u32[]{:S(2)}) collective-permute-start(bf16[128,128]{1,0:T(8,128)(2,1)S(1)} %get-tuple-element.15), channel_id=1, source_target_pairs={{16,0},{32,16},{48,32},{64,48},{80,64},{96,80},{112,96},{128,112},... | collective-permute-start | bytes 98312 | tf_op jit(solution)/shard_map/ppermute | solution.py:227
  45.9 1.0 %copy-start.1 = (f32[4,128,128]{2,1,0:T(8,128)S(1)}, f32[4,128,128]{2,1,0:T(8,128)}, u32[]{:S(2)}) copy-start(f32[4,128,128]{2,1,0:T(8,128)} %psi_ref.5) | copy-start | bytes 786436
  45.9 1.7 %copy-start.2 = (bf16[4,128,2048]{2,1,0:T(8,128)(2,1)S(1)}, bf16[4,128,2048]{2,1,0:T(8,128)(2,1)}, u32[]{:S(2)}) copy-start(bf16[4,128,2048]{2,1,0:T(8,128)(2,1)} %kernel_ref.3) | copy-start | bytes 6291460
  45.9 1.7 %copy-start.3 = (f32[2,2]{1,0:T(2,128)S(1)}, f32[2,2]{1,0:T(2,128)}, u32[]{:S(2)}) copy-start(f32[2,2]{1,0:T(2,128)} %field_ref.3) | copy-start | bytes 52
  45.9 1.7 %copy-start.4 = (s32[64]{0:T(128)S(1)}, s32[64]{0:T(128)}, u32[]{:S(2)}) copy-start(s32[64]{0:T(128)} %counts_ref.3) | copy-start | bytes 772
  50.4 31.9 %collective-permute-start.3 = (bf16[128,128]{1,0:T(8,128)(2,1)S(1)}, bf16[128,128]{1,0:T(8,128)(2,1)S(1)}, u32[]{:S(2)}, u32[]{:S(2)}) collective-permute-start(bf16[128,128]{1,0:T(8,128)(2,1)S(1)} %get-tuple-element.19), channel_id=1, source_target_pairs={{0,16},{16,32},{32,48},{48,64},{64,80},{80,96},{96,112},{112,128},... | collective-permute-start | bytes 98312 | tf_op jit(solution)/shard_map/ppermute | solution.py:227
  52.3 30.0 %collective-permute-start.4 = (bf16[128,128]{1,0:T(8,128)(2,1)S(1)}, bf16[128,128]{1,0:T(8,128)(2,1)S(1)}, u32[]{:S(2)}, u32[]{:S(2)}) collective-permute-start(bf16[128,128]{1,0:T(8,128)(2,1)S(1)} %get-tuple-element.20), channel_id=1, source_target_pairs={{16,0},{32,16},{48,32},{64,48},{80,64},{96,80},{112,96},{128,112},... | collective-permute-start | bytes 98312 | tf_op jit(solution)/shard_map/ppermute | solution.py:227

commit v2 on v1

v2 whole, which is shorter than its diff:
```python
import functools

import jax
import jax.numpy as jnp
from jax import lax
from jax.experimental import pallas as pl
from jax.experimental.pallas import tpu as pltpu
from jax.sharding import PartitionSpec as P

step_length = 0.2
momentum_top = 3.0
TOP = 13
VMEM_LIMIT = 32 * 1024 * 1024


def encode(rounded, out_ref, slot):
    rows = rounded.shape[0]
    values = rounded.astype(jnp.float32)
    largest = jnp.max(jnp.abs(values), axis=0, keepdims=True)
    exponent = jnp.clip(jnp.floor(jnp.log2(jnp.maximum(largest, 1e-36))), -110.0, 127.0)
    scaled = values * jnp.exp2(TOP - exponent)
    out_ref[slot * rows : (slot + 1) * rows, :] = scaled.astype(out_ref.dtype)
    return exponent


def store_exponents(exponents, out_ref, start):
    lanes = exponents[0].shape[1]
    pad = out_ref.shape[0] - start - len(exponents)
    rows = jnp.concatenate(exponents + [jnp.zeros((pad, lanes), jnp.float32)], axis=0)
    out_ref[start:, :] = rows.astype(out_ref.dtype)


def encode_kernel(slots, length_ref, psi_in, out_ref, low_ref, high_ref, psi_ref, held_ref):
    rows = psi_ref.shape[1]
    held_ref[...] = jnp.full(held_ref.shape, length_ref[0].astype(jnp.float32)).astype(held_ref.dtype)
    exponents = []
    for slot in range(slots):
        psi_ref[slot] = psi_in[slot]
        rounded = psi_in[slot].astype(jnp.bfloat16)
        exponents.append(encode(rounded, out_ref, slot))
    store_exponents(exponents, out_ref, slots * rows)
    low_ref[...] = psi_in[0].astype(jnp.bfloat16)
    high_ref[...] = psi_in[length_ref[0] - 1].astype(jnp.bfloat16)


def insert_kernel(encoded_ref, other_ref, kernel_in, out_ref, kernel_out):
    count = encoded_ref.shape[0] - 16
    tail = encoded_ref[count:, :].astype(jnp.float32)
    row = lax.broadcasted_iota(jnp.int32, tail.shape, 0)
    tail = jnp.where(row >= 8, other_ref[0:1].astype(jnp.float32), tail)
    out_ref[count:, :] = tail.astype(out_ref.dtype)


def kernel_product(slot, rows, blocks, gathered_ref, kernel_ref, scales):
    total = None
    for pair in range(0, blocks, 2):
        pieces = []
        for block in (pair, pair + 1):
            piece = gathered_ref[block, slot * rows : (slot + 1) * rows, :]
            scale = scales[block][slot : slot + 1]
            pieces.append((piece.astype(jnp.float32) * scale).astype(jnp.bfloat16))
        part = jnp.dot(
            kernel_ref[slot, :, pair * rows : (pair + 2) * rows],
            jnp.concatenate(pieces, axis=0),
            preferred_element_type=jnp.float32,
        )
        total = part if total is None else total + part
    return total


def read_scales(start, blocks, gathered_ref):
    return [
        jnp.exp2(gathered_ref[b, start : start + 16, :].astype(jnp.float32) - TOP)
        for b in range(blocks)
    ]


def scalar(row):
    return jnp.max(row).astype(jnp.int32)


def coupling_factors(slots, waves, first, counts, lanes):
    shape = (4 * slots, lanes)
    row = lax.broadcasted_iota(jnp.int32, shape, 0)
    lane = lax.broadcasted_iota(jnp.int32, shape, 1)
    slot, kind = row >> 2, row & 3
    q = jnp.where(lane < lanes // 2, lane, lane - lanes // 2)

    def pick(offset):
        value = jnp.full(shape, counts[offset], jnp.int32)
        for s in range(1, slots):
            value = jnp.where(slot == s, counts[s + offset], value)
        return value

    is_low = (kind & 1) == 0
    is_up = kind < 2
    count = pick(1)
    source = jnp.where(is_low, pick(0), pick(2))
    wave = first + slot
    other = wave + jnp.where(is_low, -1, 1)
    present = (other >= 0) & (other < waves)
    center = (count - 1) >> 1
    p = q + ((source - 1) >> 1) - center - jnp.where(is_up, 1, -1)
    allowed = (q < count) & (p >= 0) & (p < source) & present
    n = (q - center - jnp.where(is_up, 1, 0)).astype(jnp.float32)
    v = (wave + jnp.where(is_up, jnp.where(is_low, -1, 1), 0)).astype(jnp.float32)
    rises = (kind == 0) | (kind == 3)
    top = jnp.where(rises, (v + n + 1.0) * (v + n + 2.0), (v - n) * (v - n - 1.0))
    bottom = (2.0 * v + 1.0) * jnp.where(rises, 2.0 * v + 3.0, 2.0 * v - 1.0)
    size = jnp.sqrt(jnp.maximum(top, 0.0) / jnp.maximum(bottom, 1.0))
    return jnp.where(allowed, jnp.where(rises, size, -size), 0.0)


def lane_masks(slots, held, counts, lanes):
    lane = lax.broadcasted_iota(jnp.int32, (1, lanes), 1)
    q = jnp.where(lane < lanes // 2, lane, lane - lanes // 2)
    return [(q < counts[s + 1]) & (s < held) for s in range(slots)]


def coupled(slot, slots, held, counts, factors, states, lowest, highest):
    lanes = lowest.shape[1]
    below = lowest if slot == 0 else states[slot - 1]
    above = highest if slot == slots - 1 else jnp.where(slot + 1 < held, states[slot + 1], highest)
    center = (counts[slot + 1] - 1) >> 1
    sums = []
    for change, kind in ((1, 0), (-1, 2)):
        total = None
        for source, offset in ((below, 0), (above, 1)):
            shift = ((counts[slot + 2 * offset] - 1) >> 1) - center - change
            turned = pltpu.roll(source, (2 * lanes - shift) & (lanes - 1), 1)
            row = 4 * slot + kind + offset
            term = factors[row : row + 1] * turned
            total = term if total is None else total + term
        sums.append(total)
    return sums


def flow_of(current, term, up, down, field_x, field_y, momenta, kinetic):
    lanes = current.shape[1]
    lane = lax.broadcasted_iota(jnp.int32, (1, lanes), 1)
    turn = kinetic * current + term + momenta * (field_x * (up + down))
    swapped = pltpu.roll(turn, lanes // 2, 1)
    swapped = jnp.where(lane < lanes // 2, swapped, -swapped)
    return swapped + momenta * (field_y * (down - up))


def momenta_of(rows, lanes, radial_count):
    row = lax.broadcasted_iota(jnp.int32, (rows, lanes), 0) + lax.axis_index("ka") * rows
    momenta = (row.astype(jnp.float32) + 0.5) * (momentum_top / radial_count)
    return momenta, 0.5 * (momenta * momenta)


def half_kernel(
    slots, waves, blocks, al_count,
    held_ref, counts_ref, field_ref, psi_ref, gathered_ref, below_ref, above_ref, kernel_ref,
    half_ref, out_ref, low_ref, high_ref, factor_ref,
):
    rows, lanes = psi_ref.shape[1:]
    start = slots * rows
    seen = None
    for block in range(blocks):
        row = gathered_ref[block, start : start + 16, :].astype(jnp.float32)[8:9]
        seen = row if seen is None else seen + row
    seen = scalar(seen)
    held = scalar(held_ref[0:1].astype(jnp.float32))
    first = jnp.where(2 * lax.axis_index("al") < al_count, seen, waves - held - seen)
    lane = lax.broadcasted_iota(jnp.int32, (1, lanes), 1)
    known = jnp.concatenate(
        [counts_ref[...].astype(jnp.float32), jnp.zeros((1, lanes - waves), jnp.float32)], axis=1
    )
    counts = [
        scalar(jnp.where(lane == jnp.clip(first - 1 + i, 0, waves - 1), known, 0.0))
        for i in range(slots + 2)
    ]
    factors = coupling_factors(slots, waves, first, counts, lanes)
    notes = jnp.full((16, lanes), held.astype(jnp.float32))
    line = lax.broadcasted_iota(jnp.int32, (16, lanes), 0)
    for i in range(slots + 2):
        notes = jnp.where(line == i, counts[i].astype(jnp.float32), notes)
    halves = [
        jnp.broadcast_to(0.5 * field_ref[section : section + 1, part : part + 1], (1, lanes))
        for section in range(2)
        for part in range(2)
    ]
    for i in range(2):
        notes = jnp.where(line == 8 + i, halves[2 + i], notes)
    factor_ref[...] = jnp.concatenate([factors, notes], axis=0)
    masks = lane_masks(slots, held, counts, lanes)
    momenta, kinetic = momenta_of(rows, lanes, kernel_ref.shape[2])
    scales = read_scales(start, blocks, gathered_ref)
    psi = [jnp.where(masks[s], psi_ref[s], 0.0) for s in range(slots)]
    lowest, highest = below_ref[...].astype(jnp.float32), above_ref[...].astype(jnp.float32)
    exponents = []
    for slot in range(slots):
        up, down = coupled(slot, slots, held, counts, factors, psi, lowest, highest)
        term = kernel_product(slot, rows, blocks, gathered_ref, kernel_ref, scales)
        flow = flow_of(psi[slot], term, up, down, halves[0], halves[1], momenta, kinetic)
        half = jnp.where(masks[slot], psi[slot] + (0.5 * step_length) * flow, 0.0)
        half_ref[slot] = half
        rounded = half.astype(jnp.bfloat16)
        exponents.append(encode(rounded, out_ref, slot))
        if slot == 0:
            low_ref[...] = rounded

        @pl.when(slot == held - 1)
        def _():
            high_ref[...] = rounded

    store_exponents(exponents, out_ref, start)


def product_kernel(slots, blocks, gathered_ref, kernel_ref, out_ref):
    rows = out_ref.shape[1]
    scales = read_scales(slots * rows, blocks, gathered_ref)
    for slot in range(slots):
        out_ref[slot] = kernel_product(slot, rows, blocks, gathered_ref, kernel_ref, scales)


def last_kernel(
    slots, radial_count, factor_ref, psi_ref, half_ref, term_ref, below_ref, above_ref,
    out_hbm, out_ref, sems,
):
    rows, lanes = psi_ref.shape[1:]
    base = 4 * slots
    counts = [scalar(factor_ref[base + i : base + i + 1]) for i in range(slots + 2)]
    held = scalar(factor_ref[base + slots + 2 : base + slots + 3])
    factors = factor_ref[0:base]
    fields = factor_ref[base + 8 : base + 9], factor_ref[base + 9 : base + 10]
    masks = lane_masks(slots, held, counts, lanes)
    momenta, kinetic = momenta_of(rows, lanes, radial_count)
    lowest, highest = below_ref[...].astype(jnp.float32), above_ref[...].astype(jnp.float32)
    states = [half_ref[s] for s in range(slots)]
    copies = []
    for slot in range(slots):
        up, down = coupled(slot, slots, held, counts, factors, states, lowest, highest)
        flow = flow_of(states[slot], term_ref[slot], up, down, *fields, momenta, kinetic)
        out_ref[slot] = jnp.where(masks[slot], psi_ref[slot] + step_length * flow, 0.0)
        copies.append(pltpu.make_async_copy(out_ref.at[slot], out_hbm.at[slot], sems.at[slot]))
        copies[slot].start()
    for copy in copies:
        copy.wait()


def shards(al_count, ka_count, amplitudes, kernel, block_lengths, m_counts, vector_potential):
    slots, rows, lanes = amplitudes.shape
    radial_count = kernel.shape[2]
    waves = m_counts.shape[0]
    sent_rows = slots * rows + 16
    vmem = pl.BlockSpec(memory_space=pltpu.VMEM)
    hbm = pl.BlockSpec(memory_space=pltpu.HBM)
    params = pltpu.CompilerParams(vmem_limit_bytes=VMEM_LIMIT)
    f32, bf16 = jnp.float32, jnp.bfloat16
    shape = jax.ShapeDtypeStruct
    edge = shape((rows, lanes), bf16)
    sent = shape((sent_rows, lanes), bf16)
    state = shape((slots, rows, lanes), f32)
    sems = pltpu.SemaphoreType.DMA((slots,))

    route = []
    for d in range(al_count):
        for k in range(1, ka_count):
            source = d - k if 2 * d < al_count else d + k
            if 0 <= source < al_count:
                route.append((source * ka_count + k, d * ka_count + k))
    upward = [(i, i + 1) for i in range(al_count - 1)]
    downward = [(i + 1, i) for i in range(al_count - 1)]

    def exchange(low, high):
        return lax.ppermute(high, "al", upward), lax.ppermute(low, "al", downward)

    def gather(payload):
        payload = lax.optimization_barrier(payload.astype(jnp.float16))
        everything = lax.optimization_barrier(lax.all_gather(payload, "ka", axis=0, tiled=False))
        return everything.astype(bf16)

    encoded, low, high, psi, held = pl.pallas_call(
        functools.partial(encode_kernel, slots),
        out_shape=(sent, edge, edge, state, shape((16, lanes), bf16)),
        in_specs=[pl.BlockSpec(memory_space=pltpu.SMEM), vmem],
        out_specs=(vmem,) * 5,
        compiler_params=params,
        name="encode",
    )(block_lengths, amplitudes)
    other = lax.ppermute(held, ("al", "ka"), route)
    below, above = exchange(low, high)
    encoded, kernel = pl.pallas_call(
        insert_kernel,
        out_shape=(sent, shape(kernel.shape, bf16)),
        in_specs=[vmem] * 3,
        out_specs=(vmem,) * 2,
        input_output_aliases={0: 0, 2: 1},
        compiler_params=params,
        name="insert",
    )(encoded, other, kernel)
    gathered = gather(encoded)
    half, encoded, low, high, factors = pl.pallas_call(
        functools.partial(half_kernel, slots, waves, ka_count, al_count),
        out_shape=(state, sent, edge, edge, shape((4 * slots + 16, lanes), f32)),
        in_specs=[vmem] * 8,
        out_specs=(vmem,) * 5,
        compiler_params=params,
        name="half",
    )(held, m_counts[None], vector_potential, psi, gathered, below, above, kernel)
    gathered = gather(encoded)
    below, above = exchange(low, high)
    term = pl.pallas_call(
        functools.partial(product_kernel, slots, ka_count),
        out_shape=state,
        in_specs=[vmem] * 2,
        out_specs=vmem,
        compiler_params=params,
        cost_estimate=pl.CostEstimate(
            flops=2 * slots * rows * radial_count * lanes * 8, bytes_accessed=4 * 1024 * 1024, transcendentals=0
        ),
        name="product",
    )(gathered, kernel)
    return pl.pallas_call(
        functools.partial(last_kernel, slots, radial_count),
        out_shape=state,
        in_specs=[vmem] * 6,
        out_specs=hbm,
        scratch_shapes=[pltpu.VMEM((slots, rows, lanes), f32), sems],
        compiler_params=params,
        name="last",
    )(factors, psi, half, term, below, above)


def solution(mesh):
    in_specs = (P("al", "ka", None), P("al", "ka", None), P("al"), P(), P())
    out_specs = P("al", "ka", None)
    body = functools.partial(shards, mesh.shape["al"], mesh.shape["ka"])
    return jax.shard_map(body, mesh=mesh, in_specs=in_specs, out_specs=out_specs, check_vma=False)
```

time: 85.2 us -> 81.2 us (0.953)
  Pallas kernels: 6.22 us -> 3.95 us
    pallas_call x1 -> x2, Pallas kernels: 2.53 us -> 1.33 us  [the longest x1 1.33 us: shards(): pl.pallas_call(functools.partial(last_kernel, slots, radial_count), out_s...]
    pallas_call x1, Pallas kernels: 2.79 us -> 1.77 us  [shards(): pl.pallas_call(functools.partial(half_kernel, slots, waves, ka_count, al_...]
    unnamed x10 -> x7, local copies, waits for them, and re-layouts: 2.23 us -> 1.92 us
where the time goes in v2:
time: 81.2 us; the launch traced here: 80.9 us
  blocking collectives  53.4 us (66%)
  starting transfers between devices  20 us (25%)
  Pallas kernels  3.95 us (5%)
  local copies, waits for them, and re-layouts  1.92 us (2%)
    all_gather x2, blocking collectives, gather(): lax.all_gather(payload, 'ka', axis=0, tiled=False)  53.4 us
    ppermute x4, starting transfers between devices, exchange(): return (lax.ppermute(high, 'al', upward), lax.ppermute(low, 'al', downward))  14.8 us
    ppermute x1, starting transfers between devices, shards(): other = lax.ppermute(held, ('al', 'ka'), route)  5.17 us
    unnamed x7, local copies, waits for them, and re-layouts  1.92 us
    pallas_call x1, Pallas kernels, shards(): pl.pallas_call(functools.partial(half_kernel, slots, waves, ka_count, al_...  1.77 us
  transfers between devices with their start and end apart: 5, of which 0 were waited for; matrix products, arithmetic and copies ran while one was open for 1% of the time, Pallas kernels for 1%

profile of v2, /device:TPU:57, one launch (start us, length us, event | category | flops | bytes accessed | tf_op | source)
XLA Modules:
  0.0 80.9 jit_solution(11583409147523716242)
XLA Ops:
  0.0 0.0 copy-start
  0.0 1.6 %copy.12.kernel_in = bf16[4,128,2048]{2,1,0:T(8,128)(2,1)S(1)} copy(bf16[4,128,2048]{2,1,0:T(8,128)(2,1)} %param.6) | data formatting | bytes 4194304
  2.3 0.0 copy-done
  2.3 0.1 encode.1
  2.4 5.2 %collective-permute-start = (bf16[16,128]{1,0:T(8,128)(2,1)S(1)}, bf16[16,128]{1,0:T(8,128)(2,1)S(1)}, u32[]{:S(2)}, u32[]{:S(2)}) collective-permute-start(bf16[16,128]{1,0:T(8,128)(2,1)S(1)} %get-tuple-element.17.held_ref), channel_id=1, source_target_pairs={{1,17},{17,33},{2,34},{33,49},{18,50},{3,51},{49,65},{34,66},{19,6... | collective-permute-start | bytes 12296 | tf_op jit(solution)/shard_map/ppermute | solution.py:284
  7.6 1.9 %collective-permute-start.1 = (bf16[128,128]{1,0:T(8,128)(2,1)S(1)}, bf16[128,128]{1,0:T(8,128)(2,1)S(1)}, u32[]{:S(2)}, u32[]{:S(2)}) collective-permute-start(bf16[128,128]{1,0:T(8,128)(2,1)S(1)} %get-tuple-element.21), channel_id=1, source_target_pairs={{0,16},{16,32},{32,48},{48,64},{64,80},{80,96},{96,112},{112,128},... | collective-permute-start | bytes 98312 | tf_op jit(solution)/shard_map/ppermute | solution.py:269
  9.5 5.5 %collective-permute-start.2 = (bf16[128,128]{1,0:T(8,128)(2,1)S(1)}, bf16[128,128]{1,0:T(8,128)(2,1)S(1)}, u32[]{:S(2)}, u32[]{:S(2)}) collective-permute-start(bf16[128,128]{1,0:T(8,128)(2,1)S(1)} %get-tuple-element.22), channel_id=1, source_target_pairs={{16,0},{32,16},{48,32},{64,48},{80,64},{96,80},{112,96},{128,112},... | collective-permute-start | bytes 98312 | tf_op jit(solution)/shard_map/ppermute | solution.py:269
  15.0 0.0 collective-permute-done.other_ref
  15.0 30.2 %all-gather.4 = f16[8448,128]{1,0:T(8,128)(2,1)S(1)} all-gather(f16[528,128]{1,0:T(8,128)(2,1)S(1)} %convert_element_type.12), channel_id=2, replica_groups=mesh['al'=32,'ka'=16] {'ka'}, dimensions={0}, use_global_device_ids=true | all-gather | bytes 2297856 | tf_op jit(solution)/shard_map/all_gather | solution.py:273
  45.2 0.0 copy-start.1
  45.2 0.0 copy-start.2
  45.2 0.4 convert_element_type.13.gathered_ref
  45.6 0.0 collective-permute-done.1.below_ref
  45.6 0.0 collective-permute-done.2.above_ref
  45.6 0.3 copy-done.1
  45.9 0.0 copy-done.2
  45.9 1.8 %half.1 = (f32[4,128,128]{2,1,0:T(8,128)S(1)}, bf16[528,128]{1,0:T(8,128)(2,1)S(1)}, bf16[128,128]{1,0:T(8,128)(2,1)S(1)}, bf16[128,128]{1,0:T(8,128)(2,1)S(1)}, f32[32,128]{1,0:T(8,128)S(1)}) custom-call(bf16[16,128]{1,0:T(8,128)(2,1)S(1)} %get-tuple-element.17.held_ref, s32[1,64]{1,0:T(1,128)S(1)} %bitcast.3, f32[2,2]{1,0:T(2,128)S(1)} %copy-done.1, ...), custom_call_target="tpu_custom_call" | custom-call | tf_op jit(solution)/shard_map/half/pallas_call | solution.py:296
  47.7 1.9 %collective-permute-start.3 = (bf16[128,128]{1,0:T(8,128)(2,1)S(1)}, bf16[128,128]{1,0:T(8,128)(2,1)S(1)}, u32[]{:S(2)}, u32[]{:S(2)}) collective-permute-start(bf16[128,128]{1,0:T(8,128)(2,1)S(1)} %get-tuple-element.27), channel_id=1, source_target_pairs={{0,16},{16,32},{32,48},{48,64},{64,80},{80,96},{96,112},{112,128},... | collective-permute-start | bytes 98312 | tf_op jit(solution)/shard_map/ppermute | solution.py:269
  49.6 5.5 %collective-permute-start.4 = (bf16[128,128]{1,0:T(8,128)(2,1)S(1)}, bf16[128,128]{1,0:T(8,128)(2,1)S(1)}, u32[]{:S(2)}, u32[]{:S(2)}) collective-permute-start(bf16[128,128]{1,0:T(8,128)(2,1)S(1)} %get-tuple-element.28), channel_id=1, source_target_pairs={{16,0},{32,16},{48,32},{64,48},{80,64},{96,80},{112,96},{128,112},... | collective-permute-start | bytes 98312 | tf_op jit(solution)/shard_map/ppermute | solution.py:269
  55.1 23.3 %all-gather.5 = f16[8448,128]{1,0:T(8,128)(2,1)S(1)} all-gather(f16[528,128]{1,0:T(8,128)(2,1)S(1)} %convert_element_type.14), channel_id=3, replica_groups=mesh['al'=32,'ka'=16] {'ka'}, dimensions={0}, use_global_device_ids=true | all-gather | bytes 2297856 | tf_op jit(solution)/shard_map/all_gather | solution.py:273
  78.4 0.4 convert_element_type.15.gathered_ref
  78.7 0.8 product.1.term_ref
  79.5 0.0 collective-permute-done.3.below_ref
  79.5 0.0 collective-permute-done.4.above_ref
  79.6 1.3 %last.1 = f32[4,128,128]{2,1,0:T(8,128)} custom-call(f32[32,128]{1,0:T(8,128)S(1)} %get-tuple-element.24.factor_ref, f32[4,128,128]{2,1,0:T(8,128)S(1)} %get-tuple-element.18.psi_ref, f32[4,128,128]{2,1,0:T(8,128)S(1)} %get-tuple-element.25.half_ref, f32[4,128,128]{2,1,0:T(8,128)S(1)} %product.1.term_ref, ...), custom_call_target="tpu_custom_call" | custom-call | tf_op jit(solution)/shard_map/last/pallas_call | solution.py:317
  (3 shorter events, 0.1 us)
Async XLA Ops:
  0.0 2.3 %copy-start = (f32[4,128,128]{2,1,0:T(8,128)S(1)}, f32[4,128,128]{2,1,0:T(8,128)}, u32[]{:S(2)}) copy-start(f32[4,128,128]{2,1,0:T(8,128)} %psi_in.1) | copy-start | bytes 786436
  2.4 12.6 %collective-permute-start = (bf16[16,128]{1,0:T(8,128)(2,1)S(1)}, bf16[16,128]{1,0:T(8,128)(2,1)S(1)}, u32[]{:S(2)}, u32[]{:S(2)}) collective-permute-start(bf16[16,128]{1,0:T(8,128)(2,1)S(1)} %get-tuple-element.17.held_ref), channel_id=1, source_target_pairs={{1,17},{17,33},{2,34},{33,49},{18,50},{3,51},{49,65},{34,66},{19,6... | collective-permute-start | bytes 12296 | tf_op jit(solution)/shard_map/ppermute | solution.py:284
  7.6 38.0 %collective-permute-start.1 = (bf16[128,128]{1,0:T(8,128)(2,1)S(1)}, bf16[128,128]{1,0:T(8,128)(2,1)S(1)}, u32[]{:S(2)}, u32[]{:S(2)}) collective-permute-start(bf16[128,128]{1,0:T(8,128)(2,1)S(1)} %get-tuple-element.21), channel_id=1, source_target_pairs={{0,16},{16,32},{32,48},{48,64},{64,80},{80,96},{96,112},{112,128},... | collective-permute-start | bytes 98312 | tf_op jit(solution)/shard_map/ppermute | solution.py:269
  9.5 36.1 %collective-permute-start.2 = (bf16[128,128]{1,0:T(8,128)(2,1)S(1)}, bf16[128,128]{1,0:T(8,128)(2,1)S(1)}, u32[]{:S(2)}, u32[]{:S(2)}) collective-permute-start(bf16[128,128]{1,0:T(8,128)(2,1)S(1)} %get-tuple-element.22), channel_id=1, source_target_pairs={{16,0},{32,16},{48,32},{64,48},{80,64},{96,80},{112,96},{128,112},... | collective-permute-start | bytes 98312 | tf_op jit(solution)/shard_map/ppermute | solution.py:269
  45.2 0.7 copy-start.1
  45.2 0.7 copy-start.2
  47.7 31.9 %collective-permute-start.3 = (bf16[128,128]{1,0:T(8,128)(2,1)S(1)}, bf16[128,128]{1,0:T(8,128)(2,1)S(1)}, u32[]{:S(2)}, u32[]{:S(2)}) collective-permute-start(bf16[128,128]{1,0:T(8,128)(2,1)S(1)} %get-tuple-element.27), channel_id=1, source_target_pairs={{0,16},{16,32},{32,48},{48,64},{64,80},{80,96},{96,112},{112,128},... | collective-permute-start | bytes 98312 | tf_op jit(solution)/shard_map/ppermute | solution.py:269
  49.6 30.0 %collective-permute-start.4 = (bf16[128,128]{1,0:T(8,128)(2,1)S(1)}, bf16[128,128]{1,0:T(8,128)(2,1)S(1)}, u32[]{:S(2)}, u32[]{:S(2)}) collective-permute-start(bf16[128,128]{1,0:T(8,128)(2,1)S(1)} %get-tuple-element.28), channel_id=1, source_target_pairs={{16,0},{32,16},{48,32},{64,48},{80,64},{96,80},{112,96},{128,112},... | collective-permute-start | bytes 98312 | tf_op jit(solution)/shard_map/ppermute | solution.py:269

commit v3 on v2

--- a/solution.py
+++ b/solution.py
@@ -30,7 +30,17 @@
     out_ref[start:, :] = rows.astype(out_ref.dtype)
 
 
-def encode_kernel(slots, length_ref, psi_in, out_ref, low_ref, high_ref, psi_ref, held_ref):
+def is_even():
+    return (lax.axis_index("al") & 1) == 0
+
+
+def edges_of(first_ref, second_ref):
+    first, second = first_ref[...].astype(jnp.float32), second_ref[...].astype(jnp.float32)
+    even = is_even()
+    return jnp.where(even, second, first), jnp.where(even, first, second)
+
+
+def encode_kernel(slots, length_ref, psi_in, out_ref, next_ref, other_ref, psi_ref, held_ref):
     rows = psi_ref.shape[1]
     held_ref[...] = jnp.full(held_ref.shape, length_ref[0].astype(jnp.float32)).astype(held_ref.dtype)
     exponents = []
@@ -39,8 +49,10 @@
         rounded = psi_in[slot].astype(jnp.bfloat16)
         exponents.append(encode(rounded, out_ref, slot))
     store_exponents(exponents, out_ref, slots * rows)
-    low_ref[...] = psi_in[0].astype(jnp.bfloat16)
-    high_ref[...] = psi_in[length_ref[0] - 1].astype(jnp.bfloat16)
+    high = length_ref[0] - 1
+    even = is_even()
+    next_ref[...] = psi_in[jnp.where(even, high, 0)].astype(jnp.bfloat16)
+    other_ref[...] = psi_in[jnp.where(even, 0, high)].astype(jnp.bfloat16)
 
 
 def insert_kernel(encoded_ref, other_ref, kernel_in, out_ref, kernel_out):
@@ -152,8 +164,8 @@
 
 def half_kernel(
     slots, waves, blocks, al_count,
-    held_ref, counts_ref, field_ref, psi_ref, gathered_ref, below_ref, above_ref, kernel_ref,
-    half_ref, out_ref, low_ref, high_ref, factor_ref,
+    held_ref, counts_ref, field_ref, psi_ref, gathered_ref, first_ref, second_ref, kernel_ref,
+    half_ref, out_ref, next_ref, other_ref, factor_ref,
 ):
     rows, lanes = psi_ref.shape[1:]
     start = slots * rows
@@ -189,7 +201,7 @@
     momenta, kinetic = momenta_of(rows, lanes, kernel_ref.shape[2])
     scales = read_scales(start, blocks, gathered_ref)
     psi = [jnp.where(masks[s], psi_ref[s], 0.0) for s in range(slots)]
-    lowest, highest = below_ref[...].astype(jnp.float32), above_ref[...].astype(jnp.float32)
+    lowest, highest = edges_of(first_ref, second_ref)
     exponents = []
     for slot in range(slots):
         up, down = coupled(slot, slots, held, counts, factors, psi, lowest, highest)
@@ -199,14 +211,10 @@
         half_ref[slot] = half
         rounded = half.astype(jnp.bfloat16)
         exponents.append(encode(rounded, out_ref, slot))
-        if slot == 0:
-            low_ref[...] = rounded
-
-        @pl.when(slot == held - 1)
-        def _():
-            high_ref[...] = rounded
-
     store_exponents(exponents, out_ref, start)
+    even = is_even()
+    next_ref[...] = half_ref[jnp.where(even, held - 1, 0)].astype(jnp.bfloat16)
+    other_ref[...] = half_ref[jnp.where(even, 0, held - 1)].astype(jnp.bfloat16)
 
 
 def product_kernel(slots, blocks, gathered_ref, kernel_ref, out_ref):
@@ -217,7 +225,7 @@
 
 
 def last_kernel(
-    slots, radial_count, factor_ref, psi_ref, half_ref, term_ref, below_ref, above_ref,
+    slots, radial_count, factor_ref, psi_ref, half_ref, term_ref, first_ref, second_ref,
     out_hbm, out_ref, sems,
 ):
     rows, lanes = psi_ref.shape[1:]
@@ -228,7 +236,7 @@
     fields = factor_ref[base + 8 : base + 9], factor_ref[base + 9 : base + 10]
     masks = lane_masks(slots, held, counts, lanes)
     momenta, kinetic = momenta_of(rows, lanes, radial_count)
-    lowest, highest = below_ref[...].astype(jnp.float32), above_ref[...].astype(jnp.float32)
+    lowest, highest = edges_of(first_ref, second_ref)
     states = [half_ref[s] for s in range(slots)]
     copies = []
     for slot in range(slots):
@@ -257,23 +265,23 @@
     sems = pltpu.SemaphoreType.DMA((slots,))
 
     route = []
-    for d in range(al_count):
-        for k in range(1, ka_count):
-            source = d - k if 2 * d < al_count else d + k
-            if 0 <= source < al_count:
-                route.append((source * ka_count + k, d * ka_count + k))
-    upward = [(i, i + 1) for i in range(al_count - 1)]
-    downward = [(i + 1, i) for i in range(al_count - 1)]
-
-    def exchange(low, high):
-        return lax.ppermute(high, "al", upward), lax.ppermute(low, "al", downward)
+    for target in range(al_count // 2):
+        for source in range(target):
+            route.append((source * ka_count + target, target * ka_count + source))
+            source_twin, target_twin = al_count - 1 - source, al_count - 1 - target
+            route.append((source_twin * ka_count + target, target_twin * ka_count + source))
+    def pairs(start):
+        return [(i + a, i + 1 - a) for i in range(start, al_count - 1, 2) for a in (0, 1)]
+
+    def exchange(following, other):
+        return lax.ppermute(following, "al", pairs(0)), lax.ppermute(other, "al", pairs(1))
 
     def gather(payload):
         payload = lax.optimization_barrier(payload.astype(jnp.float16))
         everything = lax.optimization_barrier(lax.all_gather(payload, "ka", axis=0, tiled=False))
         return everything.astype(bf16)
 
-    encoded, low, high, psi, held = pl.pallas_call(
+    encoded, following, other_edge, psi, held = pl.pallas_call(
         functools.partial(encode_kernel, slots),
         out_shape=(sent, edge, edge, state, shape((16, lanes), bf16)),
         in_specs=[pl.BlockSpec(memory_space=pltpu.SMEM), vmem],
@@ -282,7 +290,7 @@
         name="encode",
     )(block_lengths, amplitudes)
     other = lax.ppermute(held, ("al", "ka"), route)
-    below, above = exchange(low, high)
+    first_edge, second_edge = exchange(following, other_edge)
     encoded, kernel = pl.pallas_call(
         insert_kernel,
         out_shape=(sent, shape(kernel.shape, bf16)),
@@ -293,16 +301,16 @@
         name="insert",
     )(encoded, other, kernel)
     gathered = gather(encoded)
-    half, encoded, low, high, factors = pl.pallas_call(
+    half, encoded, following, other_edge, factors = pl.pallas_call(
         functools.partial(half_kernel, slots, waves, ka_count, al_count),
         out_shape=(state, sent, edge, edge, shape((4 * slots + 16, lanes), f32)),
         in_specs=[vmem] * 8,
         out_specs=(vmem,) * 5,
         compiler_params=params,
         name="half",
-    )(held, m_counts[None], vector_potential, psi, gathered, below, above, kernel)
+    )(held, m_counts[None], vector_potential, psi, gathered, first_edge, second_edge, kernel)
     gathered = gather(encoded)
-    below, above = exchange(low, high)
+    first_edge, second_edge = exchange(following, other_edge)
     term = pl.pallas_call(
         functools.partial(product_kernel, slots, ka_count),
         out_shape=state,
@@ -322,7 +330,7 @@
         scratch_shapes=[pltpu.VMEM((slots, rows, lanes), f32), sems],
         compiler_params=params,
         name="last",
-    )(factors, psi, half, term, below, above)
+    )(factors, psi, half, term, first_edge, second_edge)
 
 
 def solution(mesh):

time: 81.2 us -> 77.1 us (0.950)
  the two profiles are of different devices: /device:TPU:57 before, /device:TPU:41 now
where the time goes in v3:
time: 77.1 us; the launch traced here: 76.8 us
  blocking collectives  49 us (64%)
  starting transfers between devices  16.2 us (21%)
  waiting for transfers between devices  4.8 us (6%)
  Pallas kernels  3.3 us (4%)
  local copies, waits for them, and re-layouts  1.92 us (2%)
  other arithmetic  0.81 us (1%)
    all_gather x2, blocking collectives, gather(): lax.all_gather(payload, 'ka', axis=0, tiled=False)  49 us
    ppermute x2, starting transfers between devices, exchange(): lax.ppermute(other, 'al', pairs(1))  8.81 us
    ppermute x2, starting transfers between devices, exchange(): lax.ppermute(following, 'al', pairs(0))  6.14 us
    ppermute x1, waiting for transfers between devices, shards(): other = lax.ppermute(held, ('al', 'ka'), route)  4.79 us
    unnamed x7, local copies, waits for them, and re-layouts  1.92 us
  transfers between devices with their start and end apart: 5, of which 1 were waited for; matrix products, arithmetic and copies ran while one was open for 1% of the time, Pallas kernels for 1%

profile of v3, /device:TPU:41, one launch (start us, length us, event | category | flops | bytes accessed | tf_op | source)
XLA Modules:
  0.0 76.8 jit_solution(4762835612565281790)
XLA Ops:
  0.0 0.0 copy-start
  0.0 1.6 %copy.12.kernel_in = bf16[4,128,2048]{2,1,0:T(8,128)(2,1)S(1)} copy(bf16[4,128,2048]{2,1,0:T(8,128)(2,1)} %param.6) | data formatting | bytes 4194304
  2.3 0.0 copy-done
  2.3 0.1 encode.1
  2.4 1.3 %collective-permute-start = (bf16[16,128]{1,0:T(8,128)(2,1)S(1)}, bf16[16,128]{1,0:T(8,128)(2,1)S(1)}, u32[]{:S(2)}, u32[]{:S(2)}) collective-permute-start(bf16[16,128]{1,0:T(8,128)(2,1)S(1)} %get-tuple-element.17.held_ref), channel_id=1, source_target_pairs={{1,16},{497,480},{2,32},{498,464},{18,33},{482,465},{3,48},{499,44... | collective-permute-start | bytes 12296 | tf_op jit(solution)/shard_map/ppermute | solution.py:292
  3.7 3.1 %collective-permute-start.1 = (bf16[128,128]{1,0:T(8,128)(2,1)S(1)}, bf16[128,128]{1,0:T(8,128)(2,1)S(1)}, u32[]{:S(2)}, u32[]{:S(2)}) collective-permute-start(bf16[128,128]{1,0:T(8,128)(2,1)S(1)} %get-tuple-element.21), channel_id=1, source_target_pairs={{0,16},{16,0},{32,48},{48,32},{64,80},{80,64},{96,112},{112,96},{1... | collective-permute-start | bytes 98312 | tf_op jit(solution)/shard_map/ppermute | solution.py:277
  6.8 4.5 %collective-permute-start.2 = (bf16[128,128]{1,0:T(8,128)(2,1)S(1)}, bf16[128,128]{1,0:T(8,128)(2,1)S(1)}, u32[]{:S(2)}, u32[]{:S(2)}) collective-permute-start(bf16[128,128]{1,0:T(8,128)(2,1)S(1)} %get-tuple-element.22), channel_id=1, source_target_pairs={{16,32},{32,16},{48,64},{64,48},{80,96},{96,80},{112,128},{128,112... | collective-permute-start | bytes 98312 | tf_op jit(solution)/shard_map/ppermute | solution.py:277
  11.3 4.8 %collective-permute-done.other_ref = bf16[16,128]{1,0:T(8,128)(2,1)S(1)} collective-permute-done((bf16[16,128]{1,0:T(8,128)(2,1)S(1)}, bf16[16,128]{1,0:T(8,128)(2,1)S(1)}, u32[]{:S(2)}, u32[]{:S(2)}) %collective-permute-start) | collective-permute-done | bytes 4128 | tf_op jit(solution)/shard_map/ppermute | solution.py:292
  16.1 26.6 %all-gather.4 = f16[8448,128]{1,0:T(8,128)(2,1)S(1)} all-gather(f16[528,128]{1,0:T(8,128)(2,1)S(1)} %convert_element_type.12), channel_id=2, replica_groups=mesh['al'=32,'ka'=16] {'ka'}, dimensions={0}, use_global_device_ids=true | all-gather | bytes 2297856 | tf_op jit(solution)/shard_map/all_gather | solution.py:281
  42.8 0.0 copy-start.1
  42.8 0.0 copy-start.2
  42.8 0.4 convert_element_type.13.gathered_ref
  43.1 0.0 collective-permute-done.1.first_ref
  43.2 0.0 collective-permute-done.2.second_ref
  43.2 0.3 copy-done.1
  43.4 0.0 copy-done.2
  43.5 1.1 %half.1 = (f32[4,128,128]{2,1,0:T(8,128)S(1)}, bf16[528,128]{1,0:T(8,128)(2,1)S(1)}, bf16[128,128]{1,0:T(8,128)(2,1)S(1)}, bf16[128,128]{1,0:T(8,128)(2,1)S(1)}, f32[32,128]{1,0:T(8,128)S(1)}) custom-call(bf16[16,128]{1,0:T(8,128)(2,1)S(1)} %get-tuple-element.17.held_ref, s32[1,64]{1,0:T(1,128)S(1)} %bitcast.3, f32[2,2]{1,0:T(2,128)S(1)} %copy-done.1, ...), custom_call_target="tpu_custom_call" | custom-call | tf_op jit(solution)/shard_map/half/pallas_call | solution.py:304
  44.6 3.0 %collective-permute-start.3 = (bf16[128,128]{1,0:T(8,128)(2,1)S(1)}, bf16[128,128]{1,0:T(8,128)(2,1)S(1)}, u32[]{:S(2)}, u32[]{:S(2)}) collective-permute-start(bf16[128,128]{1,0:T(8,128)(2,1)S(1)} %get-tuple-element.27), channel_id=1, source_target_pairs={{0,16},{16,0},{32,48},{48,32},{64,80},{80,64},{96,112},{112,96},{1... | collective-permute-start | bytes 98312 | tf_op jit(solution)/shard_map/ppermute | solution.py:277
  47.6 4.3 %collective-permute-start.4 = (bf16[128,128]{1,0:T(8,128)(2,1)S(1)}, bf16[128,128]{1,0:T(8,128)(2,1)S(1)}, u32[]{:S(2)}, u32[]{:S(2)}) collective-permute-start(bf16[128,128]{1,0:T(8,128)(2,1)S(1)} %get-tuple-element.28), channel_id=1, source_target_pairs={{16,32},{32,16},{48,64},{64,48},{80,96},{96,80},{112,128},{128,112... | collective-permute-start | bytes 98312 | tf_op jit(solution)/shard_map/ppermute | solution.py:277
  52.0 22.3 %all-gather.5 = f16[8448,128]{1,0:T(8,128)(2,1)S(1)} all-gather(f16[528,128]{1,0:T(8,128)(2,1)S(1)} %convert_element_type.14), channel_id=3, replica_groups=mesh['al'=32,'ka'=16] {'ka'}, dimensions={0}, use_global_device_ids=true | all-gather | bytes 2297856 | tf_op jit(solution)/shard_map/all_gather | solution.py:281
  74.3 0.4 convert_element_type.15.gathered_ref
  74.7 0.8 %product.1.term_ref = f32[4,128,128]{2,1,0:T(8,128)S(1)} custom-call(bf16[16,528,128]{2,1,0:T(8,128)(2,1)S(1)} %convert_element_type.15.gathered_ref, bf16[4,128,2048]{2,1,0:T(8,128)(2,1)S(1)} %get-tuple-element.23.kernel_ref), custom_call_target="tpu_custom_call" | custom-call | flops 2147483648 | bytes 4194304 | tf_op jit(solution)/shard_map/product/pallas_call | solution.py:314
  75.5 0.0 collective-permute-done.3.first_ref
  75.5 0.0 collective-permute-done.4.second_ref
  75.5 1.3 %last.1 = f32[4,128,128]{2,1,0:T(8,128)} custom-call(f32[32,128]{1,0:T(8,128)S(1)} %get-tuple-element.24.factor_ref, f32[4,128,128]{2,1,0:T(8,128)S(1)} %get-tuple-element.18.psi_ref, f32[4,128,128]{2,1,0:T(8,128)S(1)} %get-tuple-element.25.half_ref, f32[4,128,128]{2,1,0:T(8,128)S(1)} %product.1.term_ref, ...), custom_call_target="tpu_custom_call" | custom-call | tf_op jit(solution)/shard_map/last/pallas_call | solution.py:325
  (3 shorter events, 0.1 us)
Async XLA Ops:
  0.0 2.3 %copy-start = (f32[4,128,128]{2,1,0:T(8,128)S(1)}, f32[4,128,128]{2,1,0:T(8,128)}, u32[]{:S(2)}) copy-start(f32[4,128,128]{2,1,0:T(8,128)} %psi_in.1) | copy-start | bytes 786436
  2.4 13.7 %collective-permute-start = (bf16[16,128]{1,0:T(8,128)(2,1)S(1)}, bf16[16,128]{1,0:T(8,128)(2,1)S(1)}, u32[]{:S(2)}, u32[]{:S(2)}) collective-permute-start(bf16[16,128]{1,0:T(8,128)(2,1)S(1)} %get-tuple-element.17.held_ref), channel_id=1, source_target_pairs={{1,16},{497,480},{2,32},{498,464},{18,33},{482,465},{3,48},{499,44... | collective-permute-start | bytes 12296 | tf_op jit(solution)/shard_map/ppermute | solution.py:292
  3.7 39.5 %collective-permute-start.1 = (bf16[128,128]{1,0:T(8,128)(2,1)S(1)}, bf16[128,128]{1,0:T(8,128)(2,1)S(1)}, u32[]{:S(2)}, u32[]{:S(2)}) collective-permute-start(bf16[128,128]{1,0:T(8,128)(2,1)S(1)} %get-tuple-element.21), channel_id=1, source_target_pairs={{0,16},{16,0},{32,48},{48,32},{64,80},{80,64},{96,112},{112,96},{1... | collective-permute-start | bytes 98312 | tf_op jit(solution)/shard_map/ppermute | solution.py:277
  6.8 36.4 %collective-permute-start.2 = (bf16[128,128]{1,0:T(8,128)(2,1)S(1)}, bf16[128,128]{1,0:T(8,128)(2,1)S(1)}, u32[]{:S(2)}, u32[]{:S(2)}) collective-permute-start(bf16[128,128]{1,0:T(8,128)(2,1)S(1)} %get-tuple-element.22), channel_id=1, source_target_pairs={{16,32},{32,16},{48,64},{64,48},{80,96},{96,80},{112,128},{128,112... | collective-permute-start | bytes 98312 | tf_op jit(solution)/shard_map/ppermute | solution.py:277
  42.8 0.7 copy-start.1
  42.8 0.7 copy-start.2
  44.6 30.9 %collective-permute-start.3 = (bf16[128,128]{1,0:T(8,128)(2,1)S(1)}, bf16[128,128]{1,0:T(8,128)(2,1)S(1)}, u32[]{:S(2)}, u32[]{:S(2)}) collective-permute-start(bf16[128,128]{1,0:T(8,128)(2,1)S(1)} %get-tuple-element.27), channel_id=1, source_target_pairs={{0,16},{16,0},{32,48},{48,32},{64,80},{80,64},{96,112},{112,96},{1... | collective-permute-start | bytes 98312 | tf_op jit(solution)/shard_map/ppermute | solution.py:277
  47.6 27.9 %collective-permute-start.4 = (bf16[128,128]{1,0:T(8,128)(2,1)S(1)}, bf16[128,128]{1,0:T(8,128)(2,1)S(1)}, u32[]{:S(2)}, u32[]{:S(2)}) collective-permute-start(bf16[128,128]{1,0:T(8,128)(2,1)S(1)} %get-tuple-element.28), channel_id=1, source_target_pairs={{16,32},{32,16},{48,64},{64,48},{80,96},{96,80},{112,128},{128,112... | collective-permute-start | bytes 98312 | tf_op jit(solution)/shard_map/ppermute | solution.py:277

commit v4 on v3

--- a/solution.py
+++ b/solution.py
@@ -42,14 +42,15 @@
 
 def encode_kernel(slots, length_ref, psi_in, out_ref, next_ref, other_ref, psi_ref, held_ref):
     rows = psi_ref.shape[1]
-    held_ref[...] = jnp.full(held_ref.shape, length_ref[0].astype(jnp.float32)).astype(held_ref.dtype)
+    length = scalar(length_ref[...].astype(jnp.float32))
+    held_ref[...] = jnp.full(held_ref.shape, length.astype(jnp.float32)).astype(held_ref.dtype)
     exponents = []
     for slot in range(slots):
         psi_ref[slot] = psi_in[slot]
         rounded = psi_in[slot].astype(jnp.bfloat16)
         exponents.append(encode(rounded, out_ref, slot))
     store_exponents(exponents, out_ref, slots * rows)
-    high = length_ref[0] - 1
+    high = length - 1
     even = is_even()
     next_ref[...] = psi_in[jnp.where(even, high, 0)].astype(jnp.bfloat16)
     other_ref[...] = psi_in[jnp.where(even, 0, high)].astype(jnp.bfloat16)
@@ -284,11 +285,11 @@
     encoded, following, other_edge, psi, held = pl.pallas_call(
         functools.partial(encode_kernel, slots),
         out_shape=(sent, edge, edge, state, shape((16, lanes), bf16)),
-        in_specs=[pl.BlockSpec(memory_space=pltpu.SMEM), vmem],
+        in_specs=[vmem] * 2,
         out_specs=(vmem,) * 5,
         compiler_params=params,
         name="encode",
-    )(block_lengths, amplitudes)
+    )(block_lengths[None], amplitudes)
     other = lax.ppermute(held, ("al", "ka"), route)
     first_edge, second_edge = exchange(following, other_edge)
     encoded, kernel = pl.pallas_call(

time: 77.1 us -> 77.1 us (level)
  no operation moved by 1% of the time
where the time goes in v4:
time: 77.1 us; the launch traced here: 76.8 us
  blocking collectives  49 us (64%)
  starting transfers between devices  16.2 us (21%)
  waiting for transfers between devices  4.8 us (6%)
  Pallas kernels  3.31 us (4%)
  local copies, waits for them, and re-layouts  1.92 us (2%)
  other arithmetic  0.81 us (1%)
  between operations  0.78 us (1%)
    all_gather x2, blocking collectives, gather(): lax.all_gather(payload, 'ka', axis=0, tiled=False)  49 us
    ppermute x2, starting transfers between devices, exchange(): lax.ppermute(other, 'al', pairs(1))  8.81 us
    ppermute x2, starting transfers between devices, exchange(): lax.ppermute(following, 'al', pairs(0))  6.14 us
    ppermute x1, waiting for transfers between devices, shards(): other = lax.ppermute(held, ('al', 'ka'), route)  4.79 us
    unnamed x7, local copies, waits for them, and re-layouts  1.92 us
  transfers between devices with their start and end apart: 5, of which 1 were waited for; matrix products, arithmetic and copies ran while one was open for 1% of the time, Pallas kernels for 1%

profile of v4, /device:TPU:41, one launch (start us, length us, event | category | flops | bytes accessed | tf_op | source)
XLA Modules:
  0.0 76.8 jit_solution(11402553002682024664)
XLA Ops:
  0.0 0.0 copy-start
  0.0 1.6 %copy.12.kernel_in = bf16[4,128,2048]{2,1,0:T(8,128)(2,1)S(1)} copy(bf16[4,128,2048]{2,1,0:T(8,128)(2,1)} %param.6) | data formatting | bytes 4194304
  2.3 0.0 copy-done
  2.3 0.1 encode.1
  2.4 1.3 %collective-permute-start = (bf16[16,128]{1,0:T(8,128)(2,1)S(1)}, bf16[16,128]{1,0:T(8,128)(2,1)S(1)}, u32[]{:S(2)}, u32[]{:S(2)}) collective-permute-start(bf16[16,128]{1,0:T(8,128)(2,1)S(1)} %get-tuple-element.17.held_ref), channel_id=1, source_target_pairs={{1,16},{497,480},{2,32},{498,464},{18,33},{482,465},{3,48},{499,44... | collective-permute-start | bytes 12296 | tf_op jit(solution)/shard_map/ppermute | solution.py:293
  3.7 3.1 %collective-permute-start.1 = (bf16[128,128]{1,0:T(8,128)(2,1)S(1)}, bf16[128,128]{1,0:T(8,128)(2,1)S(1)}, u32[]{:S(2)}, u32[]{:S(2)}) collective-permute-start(bf16[128,128]{1,0:T(8,128)(2,1)S(1)} %get-tuple-element.21), channel_id=1, source_target_pairs={{0,16},{16,0},{32,48},{48,32},{64,80},{80,64},{96,112},{112,96},{1... | collective-permute-start | bytes 98312 | tf_op jit(solution)/shard_map/ppermute | solution.py:278
  6.8 4.5 %collective-permute-start.2 = (bf16[128,128]{1,0:T(8,128)(2,1)S(1)}, bf16[128,128]{1,0:T(8,128)(2,1)S(1)}, u32[]{:S(2)}, u32[]{:S(2)}) collective-permute-start(bf16[128,128]{1,0:T(8,128)(2,1)S(1)} %get-tuple-element.22), channel_id=1, source_target_pairs={{16,32},{32,16},{48,64},{64,48},{80,96},{96,80},{112,128},{128,112... | collective-permute-start | bytes 98312 | tf_op jit(solution)/shard_map/ppermute | solution.py:278
  11.3 4.8 %collective-permute-done.other_ref = bf16[16,128]{1,0:T(8,128)(2,1)S(1)} collective-permute-done((bf16[16,128]{1,0:T(8,128)(2,1)S(1)}, bf16[16,128]{1,0:T(8,128)(2,1)S(1)}, u32[]{:S(2)}, u32[]{:S(2)}) %collective-permute-start) | collective-permute-done | bytes 4128 | tf_op jit(solution)/shard_map/ppermute | solution.py:293
  16.2 26.6 %all-gather.4 = f16[8448,128]{1,0:T(8,128)(2,1)S(1)} all-gather(f16[528,128]{1,0:T(8,128)(2,1)S(1)} %convert_element_type.12), channel_id=2, replica_groups=mesh['al'=32,'ka'=16] {'ka'}, dimensions={0}, use_global_device_ids=true | all-gather | bytes 2297856 | tf_op jit(solution)/shard_map/all_gather | solution.py:282
  42.8 0.0 copy-start.1
  42.8 0.0 copy-start.2
  42.8 0.4 convert_element_type.13.gathered_ref
  43.2 0.0 collective-permute-done.1.first_ref
  43.2 0.0 collective-permute-done.2.second_ref
  43.2 0.3 copy-done.1
  43.5 0.0 copy-done.2
  43.5 1.1 %half.1 = (f32[4,128,128]{2,1,0:T(8,128)S(1)}, bf16[528,128]{1,0:T(8,128)(2,1)S(1)}, bf16[128,128]{1,0:T(8,128)(2,1)S(1)}, bf16[128,128]{1,0:T(8,128)(2,1)S(1)}, f32[32,128]{1,0:T(8,128)S(1)}) custom-call(bf16[16,128]{1,0:T(8,128)(2,1)S(1)} %get-tuple-element.17.held_ref, s32[1,64]{1,0:T(1,128)S(1)} %bitcast.5, f32[2,2]{1,0:T(2,128)S(1)} %copy-done.1, ...), custom_call_target="tpu_custom_call" | custom-call | tf_op jit(solution)/shard_map/half/pallas_call | solution.py:305
  44.6 3.0 %collective-permute-start.3 = (bf16[128,128]{1,0:T(8,128)(2,1)S(1)}, bf16[128,128]{1,0:T(8,128)(2,1)S(1)}, u32[]{:S(2)}, u32[]{:S(2)}) collective-permute-start(bf16[128,128]{1,0:T(8,128)(2,1)S(1)} %get-tuple-element.27), channel_id=1, source_target_pairs={{0,16},{16,0},{32,48},{48,32},{64,80},{80,64},{96,112},{112,96},{1... | collective-permute-start | bytes 98312 | tf_op jit(solution)/shard_map/ppermute | solution.py:278
  47.6 4.3 %collective-permute-start.4 = (bf16[128,128]{1,0:T(8,128)(2,1)S(1)}, bf16[128,128]{1,0:T(8,128)(2,1)S(1)}, u32[]{:S(2)}, u32[]{:S(2)}) collective-permute-start(bf16[128,128]{1,0:T(8,128)(2,1)S(1)} %get-tuple-element.28), channel_id=1, source_target_pairs={{16,32},{32,16},{48,64},{64,48},{80,96},{96,80},{112,128},{128,112... | collective-permute-start | bytes 98312 | tf_op jit(solution)/shard_map/ppermute | solution.py:278
  52.0 22.3 %all-gather.5 = f16[8448,128]{1,0:T(8,128)(2,1)S(1)} all-gather(f16[528,128]{1,0:T(8,128)(2,1)S(1)} %convert_element_type.14), channel_id=3, replica_groups=mesh['al'=32,'ka'=16] {'ka'}, dimensions={0}, use_global_device_ids=true | all-gather | bytes 2297856 | tf_op jit(solution)/shard_map/all_gather | solution.py:282
  74.3 0.4 convert_element_type.15.gathered_ref
  74.7 0.8 %product.1.term_ref = f32[4,128,128]{2,1,0:T(8,128)S(1)} custom-call(bf16[16,528,128]{2,1,0:T(8,128)(2,1)S(1)} %convert_element_type.15.gathered_ref, bf16[4,128,2048]{2,1,0:T(8,128)(2,1)S(1)} %get-tuple-element.23.kernel_ref), custom_call_target="tpu_custom_call" | custom-call | flops 2147483648 | bytes 4194304 | tf_op jit(solution)/shard_map/product/pallas_call | solution.py:315
  75.5 0.0 collective-permute-done.3.first_ref
  75.5 0.0 collective-permute-done.4.second_ref
  75.5 1.3 %last.1 = f32[4,128,128]{2,1,0:T(8,128)} custom-call(f32[32,128]{1,0:T(8,128)S(1)} %get-tuple-element.24.factor_ref, f32[4,128,128]{2,1,0:T(8,128)S(1)} %get-tuple-element.18.psi_ref, f32[4,128,128]{2,1,0:T(8,128)S(1)} %get-tuple-element.25.half_ref, f32[4,128,128]{2,1,0:T(8,128)S(1)} %product.1.term_ref, ...), custom_call_target="tpu_custom_call" | custom-call | tf_op jit(solution)/shard_map/last/pallas_call | solution.py:326
  (3 shorter events, 0.1 us)
Async XLA Ops:
  0.0 2.3 %copy-start = (f32[4,128,128]{2,1,0:T(8,128)S(1)}, f32[4,128,128]{2,1,0:T(8,128)}, u32[]{:S(2)}) copy-start(f32[4,128,128]{2,1,0:T(8,128)} %psi_in.1) | copy-start | bytes 786436
  2.4 13.7 %collective-permute-start = (bf16[16,128]{1,0:T(8,128)(2,1)S(1)}, bf16[16,128]{1,0:T(8,128)(2,1)S(1)}, u32[]{:S(2)}, u32[]{:S(2)}) collective-permute-start(bf16[16,128]{1,0:T(8,128)(2,1)S(1)} %get-tuple-element.17.held_ref), channel_id=1, source_target_pairs={{1,16},{497,480},{2,32},{498,464},{18,33},{482,465},{3,48},{499,44... | collective-permute-start | bytes 12296 | tf_op jit(solution)/shard_map/ppermute | solution.py:293
  3.7 39.5 %collective-permute-start.1 = (bf16[128,128]{1,0:T(8,128)(2,1)S(1)}, bf16[128,128]{1,0:T(8,128)(2,1)S(1)}, u32[]{:S(2)}, u32[]{:S(2)}) collective-permute-start(bf16[128,128]{1,0:T(8,128)(2,1)S(1)} %get-tuple-element.21), channel_id=1, source_target_pairs={{0,16},{16,0},{32,48},{48,32},{64,80},{80,64},{96,112},{112,96},{1... | collective-permute-start | bytes 98312 | tf_op jit(solution)/shard_map/ppermute | solution.py:278
  6.8 36.4 %collective-permute-start.2 = (bf16[128,128]{1,0:T(8,128)(2,1)S(1)}, bf16[128,128]{1,0:T(8,128)(2,1)S(1)}, u32[]{:S(2)}, u32[]{:S(2)}) collective-permute-start(bf16[128,128]{1,0:T(8,128)(2,1)S(1)} %get-tuple-element.22), channel_id=1, source_target_pairs={{16,32},{32,16},{48,64},{64,48},{80,96},{96,80},{112,128},{128,112... | collective-permute-start | bytes 98312 | tf_op jit(solution)/shard_map/ppermute | solution.py:278
  42.8 0.7 copy-start.1
  42.8 0.7 copy-start.2
  44.6 30.9 %collective-permute-start.3 = (bf16[128,128]{1,0:T(8,128)(2,1)S(1)}, bf16[128,128]{1,0:T(8,128)(2,1)S(1)}, u32[]{:S(2)}, u32[]{:S(2)}) collective-permute-start(bf16[128,128]{1,0:T(8,128)(2,1)S(1)} %get-tuple-element.27), channel_id=1, source_target_pairs={{0,16},{16,0},{32,48},{48,32},{64,80},{80,64},{96,112},{112,96},{1... | collective-permute-start | bytes 98312 | tf_op jit(solution)/shard_map/ppermute | solution.py:278
  47.6 27.9 %collective-permute-start.4 = (bf16[128,128]{1,0:T(8,128)(2,1)S(1)}, bf16[128,128]{1,0:T(8,128)(2,1)S(1)}, u32[]{:S(2)}, u32[]{:S(2)}) collective-permute-start(bf16[128,128]{1,0:T(8,128)(2,1)S(1)} %get-tuple-element.28), channel_id=1, source_target_pairs={{16,32},{32,16},{48,64},{64,48},{80,96},{96,80},{112,128},{128,112... | collective-permute-start | bytes 98312 | tf_op jit(solution)/shard_map/ppermute | solution.py:278

commit v5 on v4

--- a/solution.py
+++ b/solution.py
@@ -268,9 +268,9 @@
     route = []
     for target in range(al_count // 2):
         for source in range(target):
-            route.append((source * ka_count + target, target * ka_count + source))
+            route.append((source * ka_count + target - 1, target * ka_count + source))
             source_twin, target_twin = al_count - 1 - source, al_count - 1 - target
-            route.append((source_twin * ka_count + target, target_twin * ka_count + source))
+            route.append((source_twin * ka_count + target - 1, target_twin * ka_count + source))
     def pairs(start):
         return [(i + a, i + 1 - a) for i in range(start, al_count - 1, 2) for a in (0, 1)]
 

time: 77.1 us -> 77.4 us (level)
  the two profiles are of different devices: /device:TPU:41 before, /device:TPU:57 now
where the time goes in v5:
time: 77.4 us; the launch traced here: 76.9 us
  blocking collectives  52.9 us (68%)
  starting transfers between devices  17.2 us (22%)
  Pallas kernels  3.32 us (4%)
  local copies, waits for them, and re-layouts  1.92 us (2%)
  other arithmetic  0.81 us (1%)
  between operations  0.79 us (1%)
    all_gather x2, blocking collectives, gather(): lax.all_gather(payload, 'ka', axis=0, tiled=False)  52.9 us
    ppermute x2, starting transfers between devices, exchange(): lax.ppermute(other, 'al', pairs(1))  10.9 us
    ppermute x2, starting transfers between devices, exchange(): lax.ppermute(following, 'al', pairs(0))  5.04 us
    unnamed x7, local copies, waits for them, and re-layouts  1.92 us
  transfers between devices with their start and end apart: 5, of which 0 were waited for; matrix products, arithmetic and copies ran while one was open for 1% of the time, Pallas kernels for 1%

profile of v5, /device:TPU:57, one launch (start us, length us, event | category | flops | bytes accessed | tf_op | source)
XLA Modules:
  0.0 76.9 jit_solution(7419444525617748929)
XLA Ops:
  0.0 0.0 copy-start
  0.0 1.6 %copy.12.kernel_in = bf16[4,128,2048]{2,1,0:T(8,128)(2,1)S(1)} copy(bf16[4,128,2048]{2,1,0:T(8,128)(2,1)} %param.6) | data formatting | bytes 4194304
  2.3 0.0 copy-done
  2.3 0.1 encode.1
  2.4 1.3 %collective-permute-start = (bf16[16,128]{1,0:T(8,128)(2,1)S(1)}, bf16[16,128]{1,0:T(8,128)(2,1)S(1)}, u32[]{:S(2)}, u32[]{:S(2)}) collective-permute-start(bf16[16,128]{1,0:T(8,128)(2,1)S(1)} %get-tuple-element.17.held_ref), channel_id=1, source_target_pairs={{0,16},{496,480},{1,32},{497,464},{17,33},{481,465},{2,48},{498,44... | collective-permute-start | bytes 12296 | tf_op jit(solution)/shard_map/ppermute | solution.py:293
  3.7 3.1 %collective-permute-start.1 = (bf16[128,128]{1,0:T(8,128)(2,1)S(1)}, bf16[128,128]{1,0:T(8,128)(2,1)S(1)}, u32[]{:S(2)}, u32[]{:S(2)}) collective-permute-start(bf16[128,128]{1,0:T(8,128)(2,1)S(1)} %get-tuple-element.21), channel_id=1, source_target_pairs={{0,16},{16,0},{32,48},{48,32},{64,80},{80,64},{96,112},{112,96},{1... | collective-permute-start | bytes 98312 | tf_op jit(solution)/shard_map/ppermute | solution.py:278
  6.8 4.5 %collective-permute-start.2 = (bf16[128,128]{1,0:T(8,128)(2,1)S(1)}, bf16[128,128]{1,0:T(8,128)(2,1)S(1)}, u32[]{:S(2)}, u32[]{:S(2)}) collective-permute-start(bf16[128,128]{1,0:T(8,128)(2,1)S(1)} %get-tuple-element.22), channel_id=1, source_target_pairs={{16,32},{32,16},{48,64},{64,48},{80,96},{96,80},{112,128},{128,112... | collective-permute-start | bytes 98312 | tf_op jit(solution)/shard_map/ppermute | solution.py:278
  11.3 0.0 collective-permute-done.other_ref
  11.4 30.2 %all-gather.4 = f16[8448,128]{1,0:T(8,128)(2,1)S(1)} all-gather(f16[528,128]{1,0:T(8,128)(2,1)S(1)} %convert_element_type.12), channel_id=2, replica_groups=mesh['al'=32,'ka'=16] {'ka'}, dimensions={0}, use_global_device_ids=true | all-gather | bytes 2297856 | tf_op jit(solution)/shard_map/all_gather | solution.py:282
  41.6 0.0 copy-start.1
  41.6 0.0 copy-start.2
  41.6 0.4 convert_element_type.13.gathered_ref
  42.0 0.0 collective-permute-done.1.first_ref
  42.0 0.0 collective-permute-done.2.second_ref
  42.0 0.3 copy-done.1
  42.3 0.0 copy-done.2
  42.3 1.1 %half.1 = (f32[4,128,128]{2,1,0:T(8,128)S(1)}, bf16[528,128]{1,0:T(8,128)(2,1)S(1)}, bf16[128,128]{1,0:T(8,128)(2,1)S(1)}, bf16[128,128]{1,0:T(8,128)(2,1)S(1)}, f32[32,128]{1,0:T(8,128)S(1)}) custom-call(bf16[16,128]{1,0:T(8,128)(2,1)S(1)} %get-tuple-element.17.held_ref, s32[1,64]{1,0:T(1,128)S(1)} %bitcast.5, f32[2,2]{1,0:T(2,128)S(1)} %copy-done.1, ...), custom_call_target="tpu_custom_call" | custom-call | tf_op jit(solution)/shard_map/half/pallas_call | solution.py:305
  43.4 1.9 %collective-permute-start.3 = (bf16[128,128]{1,0:T(8,128)(2,1)S(1)}, bf16[128,128]{1,0:T(8,128)(2,1)S(1)}, u32[]{:S(2)}, u32[]{:S(2)}) collective-permute-start(bf16[128,128]{1,0:T(8,128)(2,1)S(1)} %get-tuple-element.27), channel_id=1, source_target_pairs={{0,16},{16,0},{32,48},{48,32},{64,80},{80,64},{96,112},{112,96},{1... | collective-permute-start | bytes 98312 | tf_op jit(solution)/shard_map/ppermute | solution.py:278
  45.3 6.4 %collective-permute-start.4 = (bf16[128,128]{1,0:T(8,128)(2,1)S(1)}, bf16[128,128]{1,0:T(8,128)(2,1)S(1)}, u32[]{:S(2)}, u32[]{:S(2)}) collective-permute-start(bf16[128,128]{1,0:T(8,128)(2,1)S(1)} %get-tuple-element.28), channel_id=1, source_target_pairs={{16,32},{32,16},{48,64},{64,48},{80,96},{96,80},{112,128},{128,112... | collective-permute-start | bytes 98312 | tf_op jit(solution)/shard_map/ppermute | solution.py:278
  51.7 22.7 %all-gather.5 = f16[8448,128]{1,0:T(8,128)(2,1)S(1)} all-gather(f16[528,128]{1,0:T(8,128)(2,1)S(1)} %convert_element_type.14), channel_id=3, replica_groups=mesh['al'=32,'ka'=16] {'ka'}, dimensions={0}, use_global_device_ids=true | all-gather | bytes 2297856 | tf_op jit(solution)/shard_map/all_gather | solution.py:282
  74.4 0.4 convert_element_type.15.gathered_ref
  74.8 0.8 %product.1.term_ref = f32[4,128,128]{2,1,0:T(8,128)S(1)} custom-call(bf16[16,528,128]{2,1,0:T(8,128)(2,1)S(1)} %convert_element_type.15.gathered_ref, bf16[4,128,2048]{2,1,0:T(8,128)(2,1)S(1)} %get-tuple-element.23.kernel_ref), custom_call_target="tpu_custom_call" | custom-call | flops 2147483648 | bytes 4194304 | tf_op jit(solution)/shard_map/product/pallas_call | solution.py:315
  75.6 0.0 collective-permute-done.3.first_ref
  75.6 0.0 collective-permute-done.4.second_ref
  75.6 1.3 %last.1 = f32[4,128,128]{2,1,0:T(8,128)} custom-call(f32[32,128]{1,0:T(8,128)S(1)} %get-tuple-element.24.factor_ref, f32[4,128,128]{2,1,0:T(8,128)S(1)} %get-tuple-element.18.psi_ref, f32[4,128,128]{2,1,0:T(8,128)S(1)} %get-tuple-element.25.half_ref, f32[4,128,128]{2,1,0:T(8,128)S(1)} %product.1.term_ref, ...), custom_call_target="tpu_custom_call" | custom-call | tf_op jit(solution)/shard_map/last/pallas_call | solution.py:326
  (3 shorter events, 0.1 us)
Async XLA Ops:
  0.0 2.3 %copy-start = (f32[4,128,128]{2,1,0:T(8,128)S(1)}, f32[4,128,128]{2,1,0:T(8,128)}, u32[]{:S(2)}) copy-start(f32[4,128,128]{2,1,0:T(8,128)} %psi_in.1) | copy-start | bytes 786436
  2.4 8.9 %collective-permute-start = (bf16[16,128]{1,0:T(8,128)(2,1)S(1)}, bf16[16,128]{1,0:T(8,128)(2,1)S(1)}, u32[]{:S(2)}, u32[]{:S(2)}) collective-permute-start(bf16[16,128]{1,0:T(8,128)(2,1)S(1)} %get-tuple-element.17.held_ref), channel_id=1, source_target_pairs={{0,16},{496,480},{1,32},{497,464},{17,33},{481,465},{2,48},{498,44... | collective-permute-start | bytes 12296 | tf_op jit(solution)/shard_map/ppermute | solution.py:293
  3.7 38.3 %collective-permute-start.1 = (bf16[128,128]{1,0:T(8,128)(2,1)S(1)}, bf16[128,128]{1,0:T(8,128)(2,1)S(1)}, u32[]{:S(2)}, u32[]{:S(2)}) collective-permute-start(bf16[128,128]{1,0:T(8,128)(2,1)S(1)} %get-tuple-element.21), channel_id=1, source_target_pairs={{0,16},{16,0},{32,48},{48,32},{64,80},{80,64},{96,112},{112,96},{1... | collective-permute-start | bytes 98312 | tf_op jit(solution)/shard_map/ppermute | solution.py:278
  6.8 35.2 %collective-permute-start.2 = (bf16[128,128]{1,0:T(8,128)(2,1)S(1)}, bf16[128,128]{1,0:T(8,128)(2,1)S(1)}, u32[]{:S(2)}, u32[]{:S(2)}) collective-permute-start(bf16[128,128]{1,0:T(8,128)(2,1)S(1)} %get-tuple-element.22), channel_id=1, source_target_pairs={{16,32},{32,16},{48,64},{64,48},{80,96},{96,80},{112,128},{128,112... | collective-permute-start | bytes 98312 | tf_op jit(solution)/shard_map/ppermute | solution.py:278
  41.6 0.7 copy-start.1
  41.6 0.7 copy-start.2
  43.4 32.2 %collective-permute-start.3 = (bf16[128,128]{1,0:T(8,128)(2,1)S(1)}, bf16[128,128]{1,0:T(8,128)(2,1)S(1)}, u32[]{:S(2)}, u32[]{:S(2)}) collective-permute-start(bf16[128,128]{1,0:T(8,128)(2,1)S(1)} %get-tuple-element.27), channel_id=1, source_target_pairs={{0,16},{16,0},{32,48},{48,32},{64,80},{80,64},{96,112},{112,96},{1... | collective-permute-start | bytes 98312 | tf_op jit(solution)/shard_map/ppermute | solution.py:278
  45.3 30.3 %collective-permute-start.4 = (bf16[128,128]{1,0:T(8,128)(2,1)S(1)}, bf16[128,128]{1,0:T(8,128)(2,1)S(1)}, u32[]{:S(2)}, u32[]{:S(2)}) collective-permute-start(bf16[128,128]{1,0:T(8,128)(2,1)S(1)} %get-tuple-element.28), channel_id=1, source_target_pairs={{16,32},{32,16},{48,64},{64,48},{80,96},{96,80},{112,128},{128,112... | collective-permute-start | bytes 98312 | tf_op jit(solution)/shard_map/ppermute | solution.py:278

commit v6 on v4

--- a/solution.py
+++ b/solution.py
@@ -218,15 +218,8 @@
     other_ref[...] = half_ref[jnp.where(even, 0, held - 1)].astype(jnp.bfloat16)
 
 
-def product_kernel(slots, blocks, gathered_ref, kernel_ref, out_ref):
-    rows = out_ref.shape[1]
-    scales = read_scales(slots * rows, blocks, gathered_ref)
-    for slot in range(slots):
-        out_ref[slot] = kernel_product(slot, rows, blocks, gathered_ref, kernel_ref, scales)
-
-
 def last_kernel(
-    slots, radial_count, factor_ref, psi_ref, half_ref, term_ref, first_ref, second_ref,
+    slots, blocks, radial_count, factor_ref, psi_ref, half_ref, gathered_ref, kernel_ref, first_ref, second_ref,
     out_hbm, out_ref, sems,
 ):
     rows, lanes = psi_ref.shape[1:]
@@ -239,10 +232,12 @@
     momenta, kinetic = momenta_of(rows, lanes, radial_count)
     lowest, highest = edges_of(first_ref, second_ref)
     states = [half_ref[s] for s in range(slots)]
+    scales = read_scales(slots * rows, blocks, gathered_ref)
     copies = []
     for slot in range(slots):
+        term = kernel_product(slot, rows, blocks, gathered_ref, kernel_ref, scales)
         up, down = coupled(slot, slots, held, counts, factors, states, lowest, highest)
-        flow = flow_of(states[slot], term_ref[slot], up, down, *fields, momenta, kinetic)
+        flow = flow_of(states[slot], term, up, down, *fields, momenta, kinetic)
         out_ref[slot] = jnp.where(masks[slot], psi_ref[slot] + step_length * flow, 0.0)
         copies.append(pltpu.make_async_copy(out_ref.at[slot], out_hbm.at[slot], sems.at[slot]))
         copies[slot].start()
@@ -312,26 +307,15 @@
     )(held, m_counts[None], vector_potential, psi, gathered, first_edge, second_edge, kernel)
     gathered = gather(encoded)
     first_edge, second_edge = exchange(following, other_edge)
-    term = pl.pallas_call(
-        functools.partial(product_kernel, slots, ka_count),
+    return pl.pallas_call(
+        functools.partial(last_kernel, slots, ka_count, radial_count),
         out_shape=state,
-        in_specs=[vmem] * 2,
-        out_specs=vmem,
-        compiler_params=params,
-        cost_estimate=pl.CostEstimate(
-            flops=2 * slots * rows * radial_count * lanes * 8, bytes_accessed=4 * 1024 * 1024, transcendentals=0
-        ),
-        name="product",
-    )(gathered, kernel)
-    return pl.pallas_call(
-        functools.partial(last_kernel, slots, radial_count),
-        out_shape=state,
-        in_specs=[vmem] * 6,
+        in_specs=[vmem] * 7,
         out_specs=hbm,
         scratch_shapes=[pltpu.VMEM((slots, rows, lanes), f32), sems],
         compiler_params=params,
         name="last",
-    )(factors, psi, half, term, first_edge, second_edge)
+    )(factors, psi, half, gathered, kernel, first_edge, second_edge)
 
 
 def solution(mesh):

time: 77.1 us -> 76.7 us (level)
    pallas_call x2 -> x1, Pallas kernels: 2.1 us -> 1.71 us  [shards(): pl.pallas_call(functools.partial(last_kernel, slots, ka_count, radial_cou...]
  transfers between devices with their start and end apart: 5 -> 5, of which waited for: 1 -> 1; matrix products, arithmetic and copies ran while one was open for 1% -> 1% of each run, Pallas kernels for 1% -> 0%
where the time goes in v6:
time: 76.7 us; the launch traced here: 76.4 us
  blocking collectives  49 us (64%)
  starting transfers between devices  16.2 us (21%)
  waiting for transfers between devices  4.8 us (6%)
  Pallas kernels  2.93 us (4%)
  local copies, waits for them, and re-layouts  1.92 us (3%)
  other arithmetic  0.81 us (1%)
  between operations  0.77 us (1%)
    all_gather x2, blocking collectives, gather(): lax.all_gather(payload, 'ka', axis=0, tiled=False)  49 us
    ppermute x2, starting transfers between devices, exchange(): lax.ppermute(other, 'al', pairs(1))  8.81 us
    ppermute x2, starting transfers between devices, exchange(): lax.ppermute(following, 'al', pairs(0))  6.14 us
    ppermute x1, waiting for transfers between devices, shards(): other = lax.ppermute(held, ('al', 'ka'), route)  4.79 us
    unnamed x7, local copies, waits for them, and re-layouts  1.92 us
    pallas_call x1, Pallas kernels, shards(): pl.pallas_call(functools.partial(last_kernel, slots, ka_count, radial_cou...  1.71 us
  transfers between devices with their start and end apart: 5, of which 1 were waited for; matrix products, arithmetic and copies ran while one was open for 1% of the time, Pallas kernels for 0%

profile of v6, /device:TPU:41, one launch (start us, length us, event | category | flops | bytes accessed | tf_op | source)
XLA Modules:
  0.0 76.4 jit_solution(11589962351068339357)
XLA Ops:
  0.0 0.0 copy-start
  0.0 1.6 %copy.12.kernel_in = bf16[4,128,2048]{2,1,0:T(8,128)(2,1)S(1)} copy(bf16[4,128,2048]{2,1,0:T(8,128)(2,1)} %param.6) | data formatting | bytes 4194304
  2.3 0.0 copy-done
  2.3 0.1 encode.1
  2.4 1.3 %collective-permute-start = (bf16[16,128]{1,0:T(8,128)(2,1)S(1)}, bf16[16,128]{1,0:T(8,128)(2,1)S(1)}, u32[]{:S(2)}, u32[]{:S(2)}) collective-permute-start(bf16[16,128]{1,0:T(8,128)(2,1)S(1)} %get-tuple-element.17.held_ref), channel_id=1, source_target_pairs={{1,16},{497,480},{2,32},{498,464},{18,33},{482,465},{3,48},{499,44... | collective-permute-start | bytes 12296 | tf_op jit(solution)/shard_map/ppermute | solution.py:288
  3.7 3.1 %collective-permute-start.1 = (bf16[128,128]{1,0:T(8,128)(2,1)S(1)}, bf16[128,128]{1,0:T(8,128)(2,1)S(1)}, u32[]{:S(2)}, u32[]{:S(2)}) collective-permute-start(bf16[128,128]{1,0:T(8,128)(2,1)S(1)} %get-tuple-element.21), channel_id=1, source_target_pairs={{0,16},{16,0},{32,48},{48,32},{64,80},{80,64},{96,112},{112,96},{1... | collective-permute-start | bytes 98312 | tf_op jit(solution)/shard_map/ppermute | solution.py:273
  6.8 4.5 %collective-permute-start.2 = (bf16[128,128]{1,0:T(8,128)(2,1)S(1)}, bf16[128,128]{1,0:T(8,128)(2,1)S(1)}, u32[]{:S(2)}, u32[]{:S(2)}) collective-permute-start(bf16[128,128]{1,0:T(8,128)(2,1)S(1)} %get-tuple-element.22), channel_id=1, source_target_pairs={{16,32},{32,16},{48,64},{64,48},{80,96},{96,80},{112,128},{128,112... | collective-permute-start | bytes 98312 | tf_op jit(solution)/shard_map/ppermute | solution.py:273
  11.3 4.8 %collective-permute-done.other_ref = bf16[16,128]{1,0:T(8,128)(2,1)S(1)} collective-permute-done((bf16[16,128]{1,0:T(8,128)(2,1)S(1)}, bf16[16,128]{1,0:T(8,128)(2,1)S(1)}, u32[]{:S(2)}, u32[]{:S(2)}) %collective-permute-start) | collective-permute-done | bytes 4128 | tf_op jit(solution)/shard_map/ppermute | solution.py:288
  16.2 26.6 %all-gather.4 = f16[8448,128]{1,0:T(8,128)(2,1)S(1)} all-gather(f16[528,128]{1,0:T(8,128)(2,1)S(1)} %convert_element_type.12), channel_id=2, replica_groups=mesh['al'=32,'ka'=16] {'ka'}, dimensions={0}, use_global_device_ids=true | all-gather | bytes 2297856 | tf_op jit(solution)/shard_map/all_gather | solution.py:277
  42.8 0.0 copy-start.1
  42.8 0.0 copy-start.2
  42.8 0.4 convert_element_type.13.gathered_ref
  43.2 0.0 collective-permute-done.1.first_ref
  43.2 0.0 collective-permute-done.2.second_ref
  43.2 0.3 copy-done.1
  43.5 0.0 copy-done.2
  43.5 1.1 %half.1 = (f32[4,128,128]{2,1,0:T(8,128)S(1)}, bf16[528,128]{1,0:T(8,128)(2,1)S(1)}, bf16[128,128]{1,0:T(8,128)(2,1)S(1)}, bf16[128,128]{1,0:T(8,128)(2,1)S(1)}, f32[32,128]{1,0:T(8,128)S(1)}) custom-call(bf16[16,128]{1,0:T(8,128)(2,1)S(1)} %get-tuple-element.17.held_ref, s32[1,64]{1,0:T(1,128)S(1)} %bitcast.5, f32[2,2]{1,0:T(2,128)S(1)} %copy-done.1, ...), custom_call_target="tpu_custom_call" | custom-call | tf_op jit(solution)/shard_map/half/pallas_call | solution.py:300
  44.6 3.0 %collective-permute-start.3 = (bf16[128,128]{1,0:T(8,128)(2,1)S(1)}, bf16[128,128]{1,0:T(8,128)(2,1)S(1)}, u32[]{:S(2)}, u32[]{:S(2)}) collective-permute-start(bf16[128,128]{1,0:T(8,128)(2,1)S(1)} %get-tuple-element.27), channel_id=1, source_target_pairs={{0,16},{16,0},{32,48},{48,32},{64,80},{80,64},{96,112},{112,96},{1... | collective-permute-start | bytes 98312 | tf_op jit(solution)/shard_map/ppermute | solution.py:273
  47.6 4.3 %collective-permute-start.4 = (bf16[128,128]{1,0:T(8,128)(2,1)S(1)}, bf16[128,128]{1,0:T(8,128)(2,1)S(1)}, u32[]{:S(2)}, u32[]{:S(2)}) collective-permute-start(bf16[128,128]{1,0:T(8,128)(2,1)S(1)} %get-tuple-element.28), channel_id=1, source_target_pairs={{16,32},{32,16},{48,64},{64,48},{80,96},{96,80},{112,128},{128,112... | collective-permute-start | bytes 98312 | tf_op jit(solution)/shard_map/ppermute | solution.py:273
  52.0 22.3 %all-gather.5 = f16[8448,128]{1,0:T(8,128)(2,1)S(1)} all-gather(f16[528,128]{1,0:T(8,128)(2,1)S(1)} %convert_element_type.14), channel_id=3, replica_groups=mesh['al'=32,'ka'=16] {'ka'}, dimensions={0}, use_global_device_ids=true | all-gather | bytes 2297856 | tf_op jit(solution)/shard_map/all_gather | solution.py:277
  74.3 0.4 convert_element_type.15.gathered_ref
  74.7 0.0 collective-permute-done.3.first_ref
  74.7 0.0 collective-permute-done.4.second_ref
  74.7 1.7 %last.1 = f32[4,128,128]{2,1,0:T(8,128)} custom-call(f32[32,128]{1,0:T(8,128)S(1)} %get-tuple-element.24.factor_ref, f32[4,128,128]{2,1,0:T(8,128)S(1)} %get-tuple-element.18.psi_ref, f32[4,128,128]{2,1,0:T(8,128)S(1)} %get-tuple-element.25.half_ref, bf16[16,528,128]{2,1,0:T(8,128)(2,1)S(1)} %convert_element_type.15.gathered_ref, ...), custom_call_target="tpu_custom_call" | custom-call | tf_op jit(solution)/shard_map/last/pallas_call | solution.py:310
  (3 shorter events, 0.1 us)
Async XLA Ops:
  0.0 2.3 %copy-start = (f32[4,128,128]{2,1,0:T(8,128)S(1)}, f32[4,128,128]{2,1,0:T(8,128)}, u32[]{:S(2)}) copy-start(f32[4,128,128]{2,1,0:T(8,128)} %psi_in.1) | copy-start | bytes 786436
  2.4 13.7 %collective-permute-start = (bf16[16,128]{1,0:T(8,128)(2,1)S(1)}, bf16[16,128]{1,0:T(8,128)(2,1)S(1)}, u32[]{:S(2)}, u32[]{:S(2)}) collective-permute-start(bf16[16,128]{1,0:T(8,128)(2,1)S(1)} %get-tuple-element.17.held_ref), channel_id=1, source_target_pairs={{1,16},{497,480},{2,32},{498,464},{18,33},{482,465},{3,48},{499,44... | collective-permute-start | bytes 12296 | tf_op jit(solution)/shard_map/ppermute | solution.py:288
  3.7 39.5 %collective-permute-start.1 = (bf16[128,128]{1,0:T(8,128)(2,1)S(1)}, bf16[128,128]{1,0:T(8,128)(2,1)S(1)}, u32[]{:S(2)}, u32[]{:S(2)}) collective-permute-start(bf16[128,128]{1,0:T(8,128)(2,1)S(1)} %get-tuple-element.21), channel_id=1, source_target_pairs={{0,16},{16,0},{32,48},{48,32},{64,80},{80,64},{96,112},{112,96},{1... | collective-permute-start | bytes 98312 | tf_op jit(solution)/shard_map/ppermute | solution.py:273
  6.8 36.4 %collective-permute-start.2 = (bf16[128,128]{1,0:T(8,128)(2,1)S(1)}, bf16[128,128]{1,0:T(8,128)(2,1)S(1)}, u32[]{:S(2)}, u32[]{:S(2)}) collective-permute-start(bf16[128,128]{1,0:T(8,128)(2,1)S(1)} %get-tuple-element.22), channel_id=1, source_target_pairs={{16,32},{32,16},{48,64},{64,48},{80,96},{96,80},{112,128},{128,112... | collective-permute-start | bytes 98312 | tf_op jit(solution)/shard_map/ppermute | solution.py:273
  42.8 0.7 copy-start.1
  42.8 0.7 copy-start.2
  44.6 30.1 %collective-permute-start.3 = (bf16[128,128]{1,0:T(8,128)(2,1)S(1)}, bf16[128,128]{1,0:T(8,128)(2,1)S(1)}, u32[]{:S(2)}, u32[]{:S(2)}) collective-permute-start(bf16[128,128]{1,0:T(8,128)(2,1)S(1)} %get-tuple-element.27), channel_id=1, source_target_pairs={{0,16},{16,0},{32,48},{48,32},{64,80},{80,64},{96,112},{112,96},{1... | collective-permute-start | bytes 98312 | tf_op jit(solution)/shard_map/ppermute | solution.py:273
  47.6 27.1 %collective-permute-start.4 = (bf16[128,128]{1,0:T(8,128)(2,1)S(1)}, bf16[128,128]{1,0:T(8,128)(2,1)S(1)}, u32[]{:S(2)}, u32[]{:S(2)}) collective-permute-start(bf16[128,128]{1,0:T(8,128)(2,1)S(1)} %get-tuple-element.28), channel_id=1, source_target_pairs={{16,32},{32,16},{48,64},{64,48},{80,96},{96,80},{112,128},{128,112... | collective-permute-start | bytes 98312 | tf_op jit(solution)/shard_map/ppermute | solution.py:273
